TPU v7x, 512 devices: a whole 4x4x16 slice. The times are simulated.
512 devices in a mesh: ctx: 32 (over x, z_lo), head: 4 (over z_hi, core), roll: 4 (over y).
Axes of the slice: x: 4, y: 4, z: 16 (z_hi: 2, z_lo: 8; z = z_hi * 8 + z_lo), core: 2. Of those that a mesh axis runs over, the one named last changes fastest.
Arguments:
- queries: bfloat16 [4, 8, 256, 128], P('roll', 'head', 'ctx'), may hold values from -80 to 80
- cache_keys: bfloat16 [4, 8, 98304, 128], P('roll', 'head', 'ctx'), may hold values from -4.5 to 4.5
- cache_values: bfloat16 [4, 8, 98304, 128], P('roll', 'head', 'ctx'), may hold values from -6 to 6
- new_keys: bfloat16 [4, 8, 16, 128], P('roll', 'head'), may hold values from -12 to 12
- new_values: bfloat16 [4, 8, 16, 128], P('roll', 'head'), may hold values from -6 to 6
- lengths: int32 [4], P('roll'), may hold values from 49152 to 98304, as said below
- positions: int32 [4, 16], P('roll'), may hold values from 49152 to 98319, as said below
- out_weight: bfloat16 [16384, 16384], P('head', ('ctx', 'roll')), may hold values from -0.046875 to 0.046875
Outputs:
- projected: bfloat16 [4, 16, 16384], P('head', None, ('ctx', 'roll'))
Inputs may be any that keep to these rules, and one draw needn't show every extreme that they name: `lengths`: at least one rollout has the full 98304 slots. positions[r] is lengths[r] plus a permutation of 0 .. 15.
All inputs are finite; a program needn't handle non-finite values.
Results may differ from a plain program's by a relative error of at most 0.04.
Values may be sent and summed in bfloat16 or wider, within the bound.
No kernel may reach another device: no remote copies, remote signals or barrier semaphores. Data moves between devices by JAX's collectives and lax.ppermute only.
A program may use at most 64 MiB of HBM per device.

v0:
```python
import jax
import jax.numpy as jnp
from jax import lax
from jax.sharding import PartitionSpec as P

NEW = 16
QPK = 16


NEG = -1e30


def shifted(value, axis, steps):
    count = lax.axis_size(axis)
    pairs = [(source, (source + steps) % count) for source in range(count)]
    return lax.ppermute(value, axis, pairs)


def body(queries, cache_keys, cache_values, new_keys, new_values, lengths, positions, out_weight):
    here = lax.axis_index("ctx")
    n_ctx = lax.axis_size("ctx")
    slots = cache_keys.shape[2]
    head_size = cache_keys.shape[3]
    local_heads = cache_keys.shape[1]
    scale = 1.0 / head_size**0.5
    keys = cache_keys[0]
    values = cache_values[0]
    fresh_keys = new_keys[0]
    fresh_values = new_values[0]
    pos = positions[0]
    slot_ok = here * slots + jnp.arange(slots) < lengths[0]

    def update(state, block, first_row, use_new):
        top_old, total_old, summed_old = state
        count = block.shape[1]
        scores = jnp.einsum("krd,ksd->krs", block, keys, preferred_element_type=jnp.float32) * scale
        scores = jnp.where(slot_ok[None, None, :], scores, NEG)
        fresh = (
            jnp.einsum("krd,kud->kru", block, fresh_keys, preferred_element_type=jnp.float32)
            * scale
        )
        token = (first_row + jnp.arange(count)) // QPK
        allow = jnp.logical_and(pos[None, :] <= pos[token][:, None], use_new)
        fresh = jnp.where(allow[None], fresh, NEG)
        top = jnp.maximum(top_old, jnp.maximum(jnp.max(scores, axis=2), jnp.max(fresh, axis=2)))
        cache_weights = jnp.where(
            slot_ok[None, None, :], jnp.exp(scores - top[..., None]), 0.0
        ).astype(jnp.bfloat16)
        fresh_weights = jnp.where(allow[None], jnp.exp(fresh - top[..., None]), 0.0).astype(
            jnp.bfloat16
        )
        factor = jnp.exp(top_old - top)
        total = total_old * factor + jnp.sum(cache_weights.astype(jnp.float32), axis=2)
        total = total + jnp.sum(fresh_weights.astype(jnp.float32), axis=2)
        summed = summed_old * factor[..., None]
        summed = summed + jnp.einsum(
            "krs,ksd->krd", cache_weights, values, preferred_element_type=jnp.float32
        )
        summed = summed + jnp.einsum(
            "kru,kud->krd", fresh_weights, fresh_values, preferred_element_type=jnp.float32
        )
        return (top, total, summed)

    block = queries[0]
    block_rows = block.shape[1]
    state = update(
        (
            jnp.full((local_heads, block_rows), NEG, jnp.float32),
            jnp.zeros((local_heads, block_rows), jnp.float32),
            jnp.zeros((local_heads, block_rows, head_size), jnp.float32),
        ),
        block,
        here * block_rows,
        True,
    )

    def turn(step, carry):
        moving, top, total, summed = carry
        moving = shifted(moving, "ctx", 1)
        top, total, summed = shifted((top, total, summed), "ctx", 1)
        top, total, summed = update((top, total, summed), moving, 0, False)
        return (moving, top, total, summed)

    moving, top, total, summed = lax.fori_loop(
        0, n_ctx - 1, turn, (block, state[0], state[1], state[2])
    )
    attended = (summed / total[..., None]).astype(jnp.bfloat16)
    every = lax.all_gather(attended[None], ("ctx", "roll"), axis=0, tiled=True)
    n_roll = every.shape[0] // n_ctx
    every = every.reshape(n_ctx, n_roll, local_heads, block_rows, head_size)
    every = jnp.roll(every, 1, axis=0)
    rows_all = every.transpose(1, 2, 0, 3, 4).reshape(
        n_roll, local_heads, n_ctx * block_rows, head_size
    )
    n_roll = rows_all.shape[0]
    features = rows_all.reshape(n_roll, local_heads, NEW, QPK, head_size).transpose(0, 2, 1, 3, 4)
    features = features.reshape(n_roll, NEW, local_heads * QPK * head_size)
    return lax.psum_scatter(
        jnp.einsum("rtf,fc->rtc", features, out_weight, preferred_element_type=jnp.float32).astype(
            jnp.bfloat16
        ),
        "head",
        scatter_dimension=0,
        tiled=True,
    )


def solution(mesh):
    in_specs = (
        P("roll", "head", "ctx", None),
        P("roll", "head", "ctx", None),
        P("roll", "head", "ctx", None),
        P("roll", "head", None, None),
        P("roll", "head", None, None),
        P("roll"),
        P("roll", None),
        P("head", ("ctx", "roll")),
    )
    out_specs = P("head", None, ("ctx", "roll"))
    return jax.shard_map(body, mesh=mesh, in_specs=in_specs, out_specs=out_specs, check_vma=False)
```

profile of v0, /device:TPU:1, one launch (start us, length us, event | category | flops | bytes accessed | tf_op | source)
XLA Modules:
  0.0 1226.3 jit_solution(11314249492497489546)
XLA Ops:
  15.0 603.7 %while.22 = (s32[]{:T(128)}, bf16[2,8,128]{2,1,0:T(8,128)(2,1)S(1)}, f32[2,8]{1,0:T(2,128)S(1)}, f32[2,8]{1,0:T(2,128)S(1)}, f32[2,8,128]{2,1,0:T(8,128)S(1)}, /...) while((s32[]{:T(128)}, ...), condition=%wide.region_7.8_spmd.clone, body=%wide.region_4.7_spmd.clone.sunk | while | flops 25718832 | bytes 10127025 | solution.py:84
  86.9 8.5 collective-permute-done
  106.2 8.5 collective-permute-done
  125.4 8.5 collective-permute-done
  144.7 8.5 collective-permute-done
  164.0 8.5 collective-permute-done
  183.2 8.5 collective-permute-done
  202.5 8.5 collective-permute-done
  221.8 8.5 collective-permute-done
  241.1 8.5 collective-permute-done
  260.3 8.5 collective-permute-done
  279.6 8.5 collective-permute-done
  298.9 8.5 collective-permute-done
  318.1 8.5 collective-permute-done
  337.4 8.8 collective-permute-done
  357.0 8.5 collective-permute-done
  395.8 8.5 collective-permute-done
  434.3 8.5 collective-permute-done
  492.2 8.5 collective-permute-done
  530.7 8.5 collective-permute-done
  550.0 8.5 collective-permute-done
  588.5 8.5 collective-permute-done
  618.7 461.5 %all-gather = bf16[256,8,128]{2,1,0:T(8,128)(2,1)S(1)} all-gather(bf16[2,8,128]{2,1,0:T(8,128)(2,1)S(1)} %divide_convert_fusion), channel_id=2, replica_groups=mesh['ctx'=32,'head'=4,'roll'=4] {'ctx','roll'}, dimensions={0}, use_global_device_ids=true | all-gather | bytes 528384 | tf_op jit(solution)/shard_map/all_gather | solution.py:88
  1081.7 137.8 %reduce-scatter.2.cloned.1.call-done = bf16[1,16,128]{2,1,0:T(8,128)(2,1)} async-done(((bf16[4,16,128]{2,1,0:T(8,128)(2,1)}), bf16[1,16,128]{2,1,0:T(8,128)(2,1)}) %reduce-scatter.2.cloned.1.call-update) | async-done | bytes 4112 | tf_op jit(solution)/shard_map/reduce_scatter | solution.py:98
  (539 shorter events, 431.3 us)
Async XLA Ops:
  6.5 1213.0 %reduce-scatter.2.cloned.1.call-start = ((), (), s32[]{:S(2)}) async-start(), calls=%async_computation.1 | async-start | bytes 20480 | tf_op jit(solution)/shard_map/reduce_scatter | solution.py:98
  15.0 21.8 %collective-permute-start.2 = (f32[2,8]{1,0:T(2,128)S(1)}, f32[2,8]{1,0:T(2,128)S(1)}, u32[]{:S(2)}, u32[]{:S(2)}) collective-permute-start(f32[2,8]{1,0:T(2,128)S(1)} %get-tuple-element.338), channel_id=1, source_target_pairs={{0,16},{16,32},{32,48},{48,64},{64,80},{80,96},{96,112},{112,128},... | collective-permute-start | bytes 200 | tf_op jit(solution)/shard_map/while/body/eval_jaxpr/ppermute | solution.py:16
  40.0 17.7 %collective-permute-start.2 = (f32[2,8]{1,0:T(2,128)S(1)}, f32[2,8]{1,0:T(2,128)S(1)}, u32[]{:S(2)}, u32[]{:S(2)}) collective-permute-start(f32[2,8]{1,0:T(2,128)S(1)} %get-tuple-element.338), channel_id=1, source_target_pairs={{0,16},{16,32},{32,48},{48,64},{64,80},{80,96},{96,112},{112,128},... | collective-permute-start | bytes 200 | tf_op jit(solution)/shard_map/while/body/eval_jaxpr/ppermute | solution.py:16
  59.2 17.7 %collective-permute-start.2 = (f32[2,8]{1,0:T(2,128)S(1)}, f32[2,8]{1,0:T(2,128)S(1)}, u32[]{:S(2)}, u32[]{:S(2)}) collective-permute-start(f32[2,8]{1,0:T(2,128)S(1)} %get-tuple-element.338), channel_id=1, source_target_pairs={{0,16},{16,32},{32,48},{48,64},{64,80},{80,96},{96,112},{112,128},... | collective-permute-start | bytes 200 | tf_op jit(solution)/shard_map/while/body/eval_jaxpr/ppermute | solution.py:16
  78.5 17.7 %collective-permute-start.2 = (f32[2,8]{1,0:T(2,128)S(1)}, f32[2,8]{1,0:T(2,128)S(1)}, u32[]{:S(2)}, u32[]{:S(2)}) collective-permute-start(f32[2,8]{1,0:T(2,128)S(1)} %get-tuple-element.338), channel_id=1, source_target_pairs={{0,16},{16,32},{32,48},{48,64},{64,80},{80,96},{96,112},{112,128},... | collective-permute-start | bytes 200 | tf_op jit(solution)/shard_map/while/body/eval_jaxpr/ppermute | solution.py:16
  97.8 17.7 %collective-permute-start.2 = (f32[2,8]{1,0:T(2,128)S(1)}, f32[2,8]{1,0:T(2,128)S(1)}, u32[]{:S(2)}, u32[]{:S(2)}) collective-permute-start(f32[2,8]{1,0:T(2,128)S(1)} %get-tuple-element.338), channel_id=1, source_target_pairs={{0,16},{16,32},{32,48},{48,64},{64,80},{80,96},{96,112},{112,128},... | collective-permute-start | bytes 200 | tf_op jit(solution)/shard_map/while/body/eval_jaxpr/ppermute | solution.py:16
  117.1 17.7 %collective-permute-start.2 = (f32[2,8]{1,0:T(2,128)S(1)}, f32[2,8]{1,0:T(2,128)S(1)}, u32[]{:S(2)}, u32[]{:S(2)}) collective-permute-start(f32[2,8]{1,0:T(2,128)S(1)} %get-tuple-element.338), channel_id=1, source_target_pairs={{0,16},{16,32},{32,48},{48,64},{64,80},{80,96},{96,112},{112,128},... | collective-permute-start | bytes 200 | tf_op jit(solution)/shard_map/while/body/eval_jaxpr/ppermute | solution.py:16
  136.3 17.7 %collective-permute-start.2 = (f32[2,8]{1,0:T(2,128)S(1)}, f32[2,8]{1,0:T(2,128)S(1)}, u32[]{:S(2)}, u32[]{:S(2)}) collective-permute-start(f32[2,8]{1,0:T(2,128)S(1)} %get-tuple-element.338), channel_id=1, source_target_pairs={{0,16},{16,32},{32,48},{48,64},{64,80},{80,96},{96,112},{112,128},... | collective-permute-start | bytes 200 | tf_op jit(solution)/shard_map/while/body/eval_jaxpr/ppermute | solution.py:16
  174.9 17.7 %collective-permute-start.2 = (f32[2,8]{1,0:T(2,128)S(1)}, f32[2,8]{1,0:T(2,128)S(1)}, u32[]{:S(2)}, u32[]{:S(2)}) collective-permute-start(f32[2,8]{1,0:T(2,128)S(1)} %get-tuple-element.338), channel_id=1, source_target_pairs={{0,16},{16,32},{32,48},{48,64},{64,80},{80,96},{96,112},{112,128},... | collective-permute-start | bytes 200 | tf_op jit(solution)/shard_map/while/body/eval_jaxpr/ppermute | solution.py:16
  194.1 17.7 %collective-permute-start.2 = (f32[2,8]{1,0:T(2,128)S(1)}, f32[2,8]{1,0:T(2,128)S(1)}, u32[]{:S(2)}, u32[]{:S(2)}) collective-permute-start(f32[2,8]{1,0:T(2,128)S(1)} %get-tuple-element.338), channel_id=1, source_target_pairs={{0,16},{16,32},{32,48},{48,64},{64,80},{80,96},{96,112},{112,128},... | collective-permute-start | bytes 200 | tf_op jit(solution)/shard_map/while/body/eval_jaxpr/ppermute | solution.py:16
  213.4 17.7 %collective-permute-start.2 = (f32[2,8]{1,0:T(2,128)S(1)}, f32[2,8]{1,0:T(2,128)S(1)}, u32[]{:S(2)}, u32[]{:S(2)}) collective-permute-start(f32[2,8]{1,0:T(2,128)S(1)} %get-tuple-element.338), channel_id=1, source_target_pairs={{0,16},{16,32},{32,48},{48,64},{64,80},{80,96},{96,112},{112,128},... | collective-permute-start | bytes 200 | tf_op jit(solution)/shard_map/while/body/eval_jaxpr/ppermute | solution.py:16
  232.7 17.7 %collective-permute-start.2 = (f32[2,8]{1,0:T(2,128)S(1)}, f32[2,8]{1,0:T(2,128)S(1)}, u32[]{:S(2)}, u32[]{:S(2)}) collective-permute-start(f32[2,8]{1,0:T(2,128)S(1)} %get-tuple-element.338), channel_id=1, source_target_pairs={{0,16},{16,32},{32,48},{48,64},{64,80},{80,96},{96,112},{112,128},... | collective-permute-start | bytes 200 | tf_op jit(solution)/shard_map/while/body/eval_jaxpr/ppermute | solution.py:16
  271.2 17.7 %collective-permute-start.2 = (f32[2,8]{1,0:T(2,128)S(1)}, f32[2,8]{1,0:T(2,128)S(1)}, u32[]{:S(2)}, u32[]{:S(2)}) collective-permute-start(f32[2,8]{1,0:T(2,128)S(1)} %get-tuple-element.338), channel_id=1, source_target_pairs={{0,16},{16,32},{32,48},{48,64},{64,80},{80,96},{96,112},{112,128},... | collective-permute-start | bytes 200 | tf_op jit(solution)/shard_map/while/body/eval_jaxpr/ppermute | solution.py:16
  290.5 17.7 %collective-permute-start.2 = (f32[2,8]{1,0:T(2,128)S(1)}, f32[2,8]{1,0:T(2,128)S(1)}, u32[]{:S(2)}, u32[]{:S(2)}) collective-permute-start(f32[2,8]{1,0:T(2,128)S(1)} %get-tuple-element.338), channel_id=1, source_target_pairs={{0,16},{16,32},{32,48},{48,64},{64,80},{80,96},{96,112},{112,128},... | collective-permute-start | bytes 200 | tf_op jit(solution)/shard_map/while/body/eval_jaxpr/ppermute | solution.py:16
  329.0 18.0 %collective-permute-start.2 = (f32[2,8]{1,0:T(2,128)S(1)}, f32[2,8]{1,0:T(2,128)S(1)}, u32[]{:S(2)}, u32[]{:S(2)}) collective-permute-start(f32[2,8]{1,0:T(2,128)S(1)} %get-tuple-element.338), channel_id=1, source_target_pairs={{0,16},{16,32},{32,48},{48,64},{64,80},{80,96},{96,112},{112,128},... | collective-permute-start | bytes 200 | tf_op jit(solution)/shard_map/while/body/eval_jaxpr/ppermute | solution.py:16
  348.6 17.7 %collective-permute-start.2 = (f32[2,8]{1,0:T(2,128)S(1)}, f32[2,8]{1,0:T(2,128)S(1)}, u32[]{:S(2)}, u32[]{:S(2)}) collective-permute-start(f32[2,8]{1,0:T(2,128)S(1)} %get-tuple-element.338), channel_id=1, source_target_pairs={{0,16},{16,32},{32,48},{48,64},{64,80},{80,96},{96,112},{112,128},... | collective-permute-start | bytes 200 | tf_op jit(solution)/shard_map/while/body/eval_jaxpr/ppermute | solution.py:16
  367.8 17.7 %collective-permute-start.2 = (f32[2,8]{1,0:T(2,128)S(1)}, f32[2,8]{1,0:T(2,128)S(1)}, u32[]{:S(2)}, u32[]{:S(2)}) collective-permute-start(f32[2,8]{1,0:T(2,128)S(1)} %get-tuple-element.338), channel_id=1, source_target_pairs={{0,16},{16,32},{32,48},{48,64},{64,80},{80,96},{96,112},{112,128},... | collective-permute-start | bytes 200 | tf_op jit(solution)/shard_map/while/body/eval_jaxpr/ppermute | solution.py:16
  406.7 17.7 %collective-permute-start.2 = (f32[2,8]{1,0:T(2,128)S(1)}, f32[2,8]{1,0:T(2,128)S(1)}, u32[]{:S(2)}, u32[]{:S(2)}) collective-permute-start(f32[2,8]{1,0:T(2,128)S(1)} %get-tuple-element.338), channel_id=1, source_target_pairs={{0,16},{16,32},{32,48},{48,64},{64,80},{80,96},{96,112},{112,128},... | collective-permute-start | bytes 200 | tf_op jit(solution)/shard_map/while/body/eval_jaxpr/ppermute | solution.py:16
  426.0 17.7 %collective-permute-start.2 = (f32[2,8]{1,0:T(2,128)S(1)}, f32[2,8]{1,0:T(2,128)S(1)}, u32[]{:S(2)}, u32[]{:S(2)}) collective-permute-start(f32[2,8]{1,0:T(2,128)S(1)} %get-tuple-element.338), channel_id=1, source_target_pairs={{0,16},{16,32},{32,48},{48,64},{64,80},{80,96},{96,112},{112,128},... | collective-permute-start | bytes 200 | tf_op jit(solution)/shard_map/while/body/eval_jaxpr/ppermute | solution.py:16
  464.5 17.7 %collective-permute-start.2 = (f32[2,8]{1,0:T(2,128)S(1)}, f32[2,8]{1,0:T(2,128)S(1)}, u32[]{:S(2)}, u32[]{:S(2)}) collective-permute-start(f32[2,8]{1,0:T(2,128)S(1)} %get-tuple-element.338), channel_id=1, source_target_pairs={{0,16},{16,32},{32,48},{48,64},{64,80},{80,96},{96,112},{112,128},... | collective-permute-start | bytes 200 | tf_op jit(solution)/shard_map/while/body/eval_jaxpr/ppermute | solution.py:16
  503.0 17.7 %collective-permute-start.2 = (f32[2,8]{1,0:T(2,128)S(1)}, f32[2,8]{1,0:T(2,128)S(1)}, u32[]{:S(2)}, u32[]{:S(2)}) collective-permute-start(f32[2,8]{1,0:T(2,128)S(1)} %get-tuple-element.338), channel_id=1, source_target_pairs={{0,16},{16,32},{32,48},{48,64},{64,80},{80,96},{96,112},{112,128},... | collective-permute-start | bytes 200 | tf_op jit(solution)/shard_map/while/body/eval_jaxpr/ppermute | solution.py:16
  522.3 17.7 %collective-permute-start.2 = (f32[2,8]{1,0:T(2,128)S(1)}, f32[2,8]{1,0:T(2,128)S(1)}, u32[]{:S(2)}, u32[]{:S(2)}) collective-permute-start(f32[2,8]{1,0:T(2,128)S(1)} %get-tuple-element.338), channel_id=1, source_target_pairs={{0,16},{16,32},{32,48},{48,64},{64,80},{80,96},{96,112},{112,128},... | collective-permute-start | bytes 200 | tf_op jit(solution)/shard_map/while/body/eval_jaxpr/ppermute | solution.py:16
  560.8 17.7 %collective-permute-start.2 = (f32[2,8]{1,0:T(2,128)S(1)}, f32[2,8]{1,0:T(2,128)S(1)}, u32[]{:S(2)}, u32[]{:S(2)}) collective-permute-start(f32[2,8]{1,0:T(2,128)S(1)} %get-tuple-element.338), channel_id=1, source_target_pairs={{0,16},{16,32},{32,48},{48,64},{64,80},{80,96},{96,112},{112,128},... | collective-permute-start | bytes 200 | tf_op jit(solution)/shard_map/while/body/eval_jaxpr/ppermute | solution.py:16
  580.1 17.7 %collective-permute-start.2 = (f32[2,8]{1,0:T(2,128)S(1)}, f32[2,8]{1,0:T(2,128)S(1)}, u32[]{:S(2)}, u32[]{:S(2)}) collective-permute-start(f32[2,8]{1,0:T(2,128)S(1)} %get-tuple-element.338), channel_id=1, source_target_pairs={{0,16},{16,32},{32,48},{48,64},{64,80},{80,96},{96,112},{112,128},... | collective-permute-start | bytes 200 | tf_op jit(solution)/shard_map/while/body/eval_jaxpr/ppermute | solution.py:16
  (136 other events, 2848.1 us)
Sparse Core Ops, SparseCore 0:
  1081.8 137.6 reduce-scatter.1
where the time goes:
time: 1230 us
  blocking collectives  462 us (38%)
  waiting for transfers between devices  435 us (35%)
  starting transfers between devices  247 us (20%)
  matrix products  35.1 us (3%)
  other arithmetic  28.6 us (2%)
  between operations  14.1 us (1%)
    all_gather x1, blocking collectives, body(): every = lax.all_gather(attended[None], ('ctx', 'roll'), axis=0, tiled=True)  462 us
    ppermute x124, waiting for transfers between devices, shifted(): return lax.ppermute(value, axis, pairs)  297 us
    ppermute x124, starting transfers between devices, shifted(): return lax.ppermute(value, axis, pairs)  247 us
    reduce_scatter x1, waiting for transfers between devices, body(): lax.psum_scatter(jnp.einsum('rtf,fc->rtc', features, out_weight, preferre...  138 us
  transfers between devices with their start and end apart: 125, of which 63 were waited for; matrix products, arithmetic and copies ran while one was open for 4% of the time, Pallas kernels for 0%

commit v1 on v0

v1 whole, which is shorter than its diff:
```python
import functools
import math

import jax
import jax.numpy as jnp
from jax import lax
from jax.experimental import pallas as pl
from jax.experimental.pallas import tpu as pltpu
from jax.sharding import Mesh
from jax.sharding import PartitionSpec as P

NEW = 16
QPK = 16
NEG = -1e30
CTX = ("x", "zl")
HEAD = ("zh", "core")
BF = jnp.bfloat16
F32 = jnp.float32
STAT_ROWS = 16


def iota(shape, dim):
    return lax.broadcasted_iota(jnp.int32, shape, dim)


def dot_nt(a, b):
    return lax.dot_general(a, b, (((1,), (1,)), ((), ())), preferred_element_type=F32)


def split3(row):
    hi = row.astype(BF).astype(F32)
    rest = row - hi
    mid = rest.astype(BF).astype(F32)
    return hi, mid, rest - mid


def pack_stats(top, total):
    rows = split3(top) + split3(total)
    at = iota((STAT_ROWS, top.shape[1]), 0)
    out = jnp.zeros((STAT_ROWS, top.shape[1]), F32)
    for n, row in enumerate(rows):
        out = jnp.where(at == n, row, out)
    return out.astype(BF)


def unpack_stats(tile):
    rows = tile.astype(F32)
    top = (rows[0:1] + rows[1:2]) + rows[2:3]
    total = (rows[3:4] + rows[4:5]) + rows[5:6]
    return top, total


def attend_kernel(info, q_ref, keys, values, fresh_keys, fresh_values, pos_ref, out_ref, scores, *, rate, chunk):
    heads, slots, size = keys.shape
    n_rows = heads * NEW * QPK
    rows = NEW * QPK
    valid = info[0]
    fresh_on = info[1]
    queries = q_ref[...].reshape(n_rows, size)
    dest = iota((n_rows, 1), 0)
    head, j, token = dest // rows, (dest // NEW) % QPK, dest % NEW
    half_rows = QPK // 2
    source = (token * 2 + j // half_rows) * (heads * half_rows) + head * half_rows + j % half_rows
    order = jnp.where(iota((n_rows, n_rows), 1) == source, 1.0, 0.0).astype(BF)
    queries = jnp.dot(order, queries, preferred_element_type=F32).astype(BF)

    pos = jnp.broadcast_to(pos_ref[...], (rows, NEW))
    mine = jnp.where(iota((rows, NEW), 0) % NEW == iota((rows, NEW), 1), pos, 0)
    allow = jnp.logical_and(pos <= jnp.sum(mine, axis=1, keepdims=True), fresh_on > 0)

    for k in range(heads):
        q = queries[k * rows : (k + 1) * rows]
        fresh = jnp.where(allow, dot_nt(q, fresh_keys[k]), NEG)
        part = jnp.full((rows, 128), NEG, F32)
        for c in range(slots // chunk):
            s = dot_nt(q, keys[k, pl.ds(c * chunk, chunk), :])
            s = jnp.where(iota((1, chunk), 1) + c * chunk < valid, s, NEG)
            scores[:, pl.ds(c * chunk, chunk)] = s
            for i in range(chunk // 128):
                part = jnp.maximum(part, s[:, i * 128 : (i + 1) * 128])
        top = jnp.maximum(jnp.max(part, axis=1, keepdims=True), jnp.max(fresh, axis=1, keepdims=True))
        weights = jnp.exp2((fresh - top) * rate).astype(BF)
        fresh_ones = jnp.concatenate([fresh_values[k], jnp.ones((NEW, size), BF)], axis=1)
        acc = jnp.dot(weights, fresh_ones, preferred_element_type=F32)
        for c in range(slots // chunk):
            w = jnp.exp2((scores[:, pl.ds(c * chunk, chunk)] - top) * rate).astype(BF)
            v = jnp.concatenate([values[k, pl.ds(c * chunk, chunk), :], jnp.ones((chunk, size), BF)], axis=1)
            acc = acc + jnp.dot(w, v, preferred_element_type=F32)
        total = acc[:, size:]
        attended = (acc[:, :size] / total).astype(BF)
        for h in range(2):
            part_rows = slice(h * 128, (h + 1) * 128)
            lane = iota((128, 128), 1)
            cols = jnp.where(lane == 0, top[part_rows], total[part_rows])
            stats = jnp.transpose(cols)
            out_ref[2 * k + h, 0:128, :] = attended[part_rows]
            out_ref[2 * k + h, 128:, :] = pack_stats(stats[0:1], stats[1:2])


def combine_kernel(r_ref, out_ref, *, rate, last):
    sources = r_ref.shape[0]
    copies = out_ref.shape[0]
    stats = [unpack_stats(r_ref[s, 128:, :]) for s in range(sources)]
    top = functools.reduce(jnp.maximum, [m for m, _ in stats])
    weights = [t * jnp.exp2((m - top) * rate) for m, t in stats]
    total = functools.reduce(jnp.add, weights)
    at = iota((128, 128), 0)
    factors = jnp.zeros((128, 128), F32)
    for s in range(sources):
        factors = jnp.where(at == s, weights[s] / total, factors)
    factors = jnp.transpose(factors)
    out = jnp.zeros((128, 128), F32)
    for s in range(sources):
        out = out + factors[:, s : s + 1] * r_ref[s, 0:128, :].astype(F32)
    out = out.astype(BF)
    for c in range(copies):
        out_ref[c, 0:128, :] = out
    if not last:
        tail = pack_stats(top, total)
        for c in range(copies):
            out_ref[c, 128:, :] = tail


def project_kernel(r_ref, w_ref, out_ref):
    n_x, n_y, rows, size = r_ref.shape
    per = rows // NEW
    acc = jnp.zeros((n_y * NEW, w_ref.shape[1]), F32)
    for x in range(n_x):
        for j in range(0, per, 2):
            block = jnp.concatenate(
                [
                    jnp.concatenate([r_ref[x, y, pl.ds((j + i) * NEW, NEW), :] for y in range(n_y)], axis=0)
                    for i in range(2)
                ],
                axis=1,
            )
            acc = acc + jnp.dot(
                block, w_ref[pl.ds((x * per + j) * size, 2 * size), :], preferred_element_type=F32
            )
    out_ref[...] = acc.astype(BF).reshape(out_ref.shape)


def in_vmem(n):
    return [pl.BlockSpec(memory_space=pltpu.VMEM)] * n


def attend(info, q, keys, values, fresh_keys, fresh_values, pos):
    heads, slots, size = keys.shape
    rate = math.log2(math.e) / size**0.5
    chunk = min(slots, 512)
    flops = 4 * heads * NEW * QPK * slots * size
    return pl.pallas_call(
        functools.partial(attend_kernel, rate=rate, chunk=chunk),
        out_shape=jax.ShapeDtypeStruct((2 * heads, 128 + STAT_ROWS, size), BF),
        in_specs=[pl.BlockSpec(memory_space=pltpu.SMEM)] + in_vmem(6),
        out_specs=pl.BlockSpec(memory_space=pltpu.VMEM),
        scratch_shapes=[pltpu.VMEM((NEW * QPK, slots), F32)],
        compiler_params=pltpu.CompilerParams(vmem_limit_bytes=24 << 20),
        cost_estimate=pl.CostEstimate(
            flops=flops, bytes_accessed=2 * heads * slots * size * 2, transcendentals=heads * NEW * QPK * slots
        ),
        name="attend",
    )(info, q, keys, values, fresh_keys, fresh_values, pos)


def combine(r, copies, last, rate):
    rows = 128 if last else 128 + STAT_ROWS
    return pl.pallas_call(
        functools.partial(combine_kernel, rate=rate, last=last),
        out_shape=jax.ShapeDtypeStruct((copies, rows, r.shape[2]), BF),
        in_specs=in_vmem(1),
        out_specs=pl.BlockSpec(memory_space=pltpu.VMEM),
        name="combine_last" if last else "combine",
    )(r)


def project(r, w):
    return pl.pallas_call(
        project_kernel,
        out_shape=jax.ShapeDtypeStruct((r.shape[1], NEW, w.shape[1]), BF),
        in_specs=in_vmem(2),
        out_specs=pl.BlockSpec(memory_space=pltpu.VMEM),
        name="project",
    )(r, w)


def body(queries, cache_keys, cache_values, new_keys, new_values, lengths, positions, out_weight):
    size = cache_keys.shape[3]
    slots = cache_keys.shape[2]
    rate = math.log2(math.e) / size**0.5
    n_ctx = lax.axis_size(CTX)
    here = lax.axis_index(CTX)
    info = jnp.stack([lengths[0] - here * slots, (here == 0).astype(jnp.int32)])
    mine = queries[0].reshape(1, -1, size)
    sent = jnp.broadcast_to(mine, (n_ctx,) + mine.shape[1:])
    q = lax.all_to_all(sent, CTX, 0, 0, tiled=True)
    part = attend(info, q, cache_keys[0], cache_values[0], new_keys[0], new_values[0], positions)
    part = lax.all_to_all(part, "x", 0, 0, tiled=True)
    part = combine(part, lax.axis_size("zl"), False, rate)
    part = lax.all_to_all(part, "zl", 0, 0, tiled=True)
    n_x, n_y = lax.axis_size("x"), lax.axis_size("y")
    rows = combine(part, n_x * n_y, True, rate)
    rows = lax.all_to_all(rows, ("x", "y"), 0, 0, tiled=True)
    out = project(rows.reshape(n_x, n_y, *rows.shape[1:]), out_weight)
    every = lax.all_gather(out, HEAD, axis=0)
    mine = lax.dynamic_index_in_dim(every, lax.axis_index(HEAD), 1, keepdims=True)
    return jnp.sum(mine.astype(F32), axis=0).astype(BF)


def solution(mesh):
    fine = Mesh(mesh.devices.reshape(4, 8, 2, 2, 4), ("x", "zl", "zh", "core", "y"))
    in_specs = (
        P("y", HEAD, CTX, None),
        P("y", HEAD, CTX, None),
        P("y", HEAD, CTX, None),
        P("y", HEAD, None, None),
        P("y", HEAD, None, None),
        P("y"),
        P("y", None),
        P(HEAD, CTX + ("y",)),
    )
    out_specs = P(HEAD, None, CTX + ("y",))
    return jax.shard_map(body, mesh=fine, in_specs=in_specs, out_specs=out_specs, check_vma=False)
```

time: 1230 us -> 110 us (0.09)
  waiting for transfers between devices: 435 us -> 20.1 us
  blocking collectives: 462 us -> 49.2 us
  starting transfers between devices: 247 us -> 21.1 us
  matrix products: 35.1 us -> 0 us
  other arithmetic: 28.6 us -> 0.67 us
  between operations: 14.1 us -> 0.69 us
    all_gather x1, blocking collectives: 462 us -> 18.9 us  [body(): every = lax.all_gather(out, HEAD, axis=0)]
    ppermute x124 -> x0, waiting for transfers between devices: 297 us -> none  [shifted(): return lax.ppermute(value, axis, pairs)]
    ppermute x124 -> x0, starting transfers between devices: 247 us -> none  [shifted(): return lax.ppermute(value, axis, pairs)]
    reduce_scatter x1 -> x0, waiting for transfers between devices: 138 us -> none  [body(): lax.psum_scatter(jnp.einsum('rtf,fc->rtc', features, out_weight, preferre...]
    dot_general x68 -> x0, matrix products: 35.1 us -> none  [the longest x32 20.5 us: update(): jnp.einsum('krd,ksd->krs', block, keys, preferred_element_type=jnp.float32)]
    all_to_all x0 -> x2, blocking collectives: none -> 30.3 us  [the longest x1 22.4 us: body(): part = lax.all_to_all(part, 'zl', 0, 0, tiled=True)]
    all_to_all x0 -> x2, starting transfers between devices: none -> 21.1 us  [the longest x1 15.9 us: body(): q = lax.all_to_all(sent, CTX, 0, 0, tiled=True)]
    lt x32 -> x0, other arithmetic: 20.3 us -> none  [body(): slot_ok = here * slots + jnp.arange(slots) < lengths[0]]
  transfers between devices with their start and end apart: 125 -> 2, of which waited for: 63 -> 2; matrix products, arithmetic and copies ran while one was open for 4% -> 0% of each run, Pallas kernels for 0% -> 0%
where the time goes in v1:
time: 110 us; the launch traced here: 109 us
  blocking collectives  49.2 us (45%)
  starting transfers between devices  21.1 us (19%)
  waiting for transfers between devices  20.1 us (18%)
  Pallas kernels  10.5 us (10%)
  local copies, waits for them, and re-layouts  7.01 us (6%)
    all_to_all x1, blocking collectives, body(): part = lax.all_to_all(part, 'zl', 0, 0, tiled=True)  22.4 us
    all_gather x1, blocking collectives, body(): every = lax.all_gather(out, HEAD, axis=0)  18.9 us
    all_to_all x1, starting transfers between devices, body(): q = lax.all_to_all(sent, CTX, 0, 0, tiled=True)  15.9 us
    all_to_all x1, waiting for transfers between devices, body(): q = lax.all_to_all(sent, CTX, 0, 0, tiled=True)  11 us
    all_to_all x1, waiting for transfers between devices, body(): rows = lax.all_to_all(rows, ('x', 'y'), 0, 0, tiled=True)  9.05 us
    all_to_all x1, blocking collectives, body(): part = lax.all_to_all(part, 'x', 0, 0, tiled=True)  7.95 us
    unnamed x12, local copies, waits for them, and re-layouts  5.65 us
    all_to_all x1, starting transfers between devices, body(): rows = lax.all_to_all(rows, ('x', 'y'), 0, 0, tiled=True)  5.15 us
  transfers between devices with their start and end apart: 2, of which 2 were waited for; matrix products, arithmetic and copies ran while one was open for 0% of the time, Pallas kernels for 0%

profile of v1, /device:TPU:1, one launch (start us, length us, event | category | flops | bytes accessed | tf_op | source)
XLA Modules:
  0.0 109.3 jit_solution(7693104150051989463)
XLA Ops:
  0.0 1.4 %broadcast_in_dim.8 = bf16[32,16,128]{2,1,0:T(8,128)(2,1)} broadcast(bf16[16,128]{1,0:T(8,128)(2,1)} %bitcast.18), dimensions={1,2} | broadcast | bytes 135168 | tf_op jit(solution)/shard_map/broadcast_in_dim | solution.py:195
  1.4 15.9 %all-to-all-start = ((bf16[32,16,128]{2,1,0:T(8,128)(2,1)}), bf16[32,16,128]{2,1,0:T(8,128)(2,1)S(1)}, u32[]{:S(2)}, u32[]{:S(2)}) async-start(bf16[32,16,128]{2,1,0:T(8,128)(2,1)} %broadcast_in_dim.8), calls=%async_computation | async-start | bytes 262144 | tf_op jit(solution)/shard_map/all_to_all | solution.py:196
  17.9 0.1 pad_add_fusion.info
  18.0 11.0 %all-to-all-done.q_ref = bf16[32,16,128]{2,1,0:T(8,128)(2,1)S(1)} async-done(((bf16[32,16,128]{2,1,0:T(8,128)(2,1)}), bf16[32,16,128]{2,1,0:T(8,128)(2,1)S(1)}, u32[]{:S(2)}, u32[]{:S(2)}) %all-to-all-start) | async-done | bytes 131104 | tf_op jit(solution)/shard_map/all_to_all | solution.py:196
  29.1 0.0 copy-start
  29.1 1.4 %copy-done = bf16[1,2,3072,128]{3,2,1,0:T(8,128)(2,1)S(1)} copy-done((bf16[1,2,3072,128]{3,2,1,0:T(8,128)(2,1)S(1)}, bf16[1,2,3072,128]{3,2,1,0:T(8,128)(2,1)}, u32[]{:S(2)}) %copy-start) | copy-done | bytes 1572888
  30.5 0.0 copy-start.1
  30.5 1.4 %copy-done.1 = bf16[1,2,3072,128]{3,2,1,0:T(8,128)(2,1)S(1)} copy-done((bf16[1,2,3072,128]{3,2,1,0:T(8,128)(2,1)S(1)}, bf16[1,2,3072,128]{3,2,1,0:T(8,128)(2,1)}, u32[]{:S(2)}) %copy-start.1) | copy-done | bytes 1572888
  31.9 0.0 copy-start.2
  31.9 0.7 copy-done.2
  32.6 0.7 copy-done.3
  33.3 0.0 copy-start.4
  33.3 0.7 copy-done.4
  33.9 4.1 %attend.1 = bf16[4,144,128]{2,1,0:T(8,128)(2,1)S(1)} custom-call(s32[2]{0:T(128)S(1)} %pad_add_fusion.info, bf16[32,16,128]{2,1,0:T(8,128)(2,1)S(1)} %all-to-all-done.q_ref, bf16[2,3072,128]{2,1,0:T(8,128)(2,1)S(1)} %bitcast.12, bf16[2,3072,128]{2,1,0:T(8,128)(2,1)S(1)} %bitcast.13, bf16[2,16,128]{2,1,0:T(8,128)(2,1)S(1)} %bitcast.14, ...), custom_call_target="tpu_custom_call" | custom-call | flops 805306368 | bytes 3145728 | tf_op jit(solution)/shard_map/attend/pallas_call | solution.py:152
  38.0 7.9 %all_to_all.20.r_ref = bf16[4,144,128]{2,1,0:T(8,128)(2,1)} all-to-all(bf16[4,144,128]{2,1,0:T(8,128)(2,1)S(1)} %attend.1), channel_id=1, replica_groups=mesh['x'=4,'zl'=8,'zh'=2,'core'=2,'y'=4] {'x'}, dimensions={0} | all-to-all | bytes 294912 | tf_op jit(solution)/shard_map/all_to_all | solution.py:198
  46.0 1.9 %combine.1 = bf16[8,144,128]{2,1,0:T(8,128)(2,1)} custom-call(bf16[4,144,128]{2,1,0:T(8,128)(2,1)} %all_to_all.20.r_ref), custom_call_target="tpu_custom_call" | custom-call | tf_op jit(solution)/shard_map/combine/pallas_call | solution.py:168
  47.9 22.4 %all_to_all.21.r_ref = bf16[8,144,128]{2,1,0:T(8,128)(2,1)} all-to-all(bf16[8,144,128]{2,1,0:T(8,128)(2,1)} %combine.1), channel_id=1, replica_groups=mesh['x'=4,'zl'=8,'zh'=2,'core'=2,'y'=4] {'zl'}, dimensions={0} | all-to-all | bytes 589824 | tf_op jit(solution)/shard_map/all_to_all | solution.py:200
  70.3 2.2 %combine_last.1 = bf16[16,128,128]{2,1,0:T(8,128)(2,1)} custom-call(bf16[8,144,128]{2,1,0:T(8,128)(2,1)} %all_to_all.21.r_ref), custom_call_target="tpu_custom_call" | custom-call | tf_op jit(solution)/shard_map/combine_last/pallas_call | solution.py:168
  72.4 5.2 %all-to-all-start.3 = ((bf16[16,128,128]{2,1,0:T(8,128)(2,1)}), bf16[16,128,128]{2,1,0:T(8,128)(2,1)S(1)}, u32[]{:S(2)}, u32[]{:S(2)}) async-start(bf16[16,128,128]{2,1,0:T(8,128)(2,1)} %combine_last.1), calls=%async_computation.3 | async-start | bytes 1048576 | tf_op jit(solution)/shard_map/all_to_all | solution.py:203
  77.6 9.0 %all-to-all-done.3 = bf16[16,128,128]{2,1,0:T(8,128)(2,1)S(1)} async-done(((bf16[16,128,128]{2,1,0:T(8,128)(2,1)}), bf16[16,128,128]{2,1,0:T(8,128)(2,1)S(1)}, u32[]{:S(2)}, u32[]{:S(2)}) %all-to-all-start.3) | async-done | bytes 524320 | tf_op jit(solution)/shard_map/all_to_all | solution.py:203
  86.7 0.8 copy-done.5
  87.5 2.3 %project.1 = bf16[4,16,128]{2,1,0:T(8,128)(2,1)} custom-call(bf16[4,4,128,128]{3,2,1,0:T(8,128)(2,1)} %bitcast.16, bf16[4096,128]{1,0:T(8,128)(2,1)} %w_ref.1), custom_call_target="tpu_custom_call" | custom-call | tf_op jit(solution)/shard_map/project/pallas_call | solution.py:178
  89.8 18.9 %all-gather = bf16[16,16,128]{2,1,0:T(8,128)(2,1)S(1)} all-gather(bf16[4,16,128]{2,1,0:T(8,128)(2,1)} %project.1), channel_id=2, replica_groups=mesh['x'=4,'zl'=8,'zh'=2,'core'=2,'y'=4] {'zh','core'}, dimensions={0}, use_global_device_ids=true | all-gather | bytes 81920 | tf_op jit(solution)/shard_map/all_gather | solution.py:205
  108.7 0.6 dynamic-slice_reduce_fusion
  (2 shorter events, 0.0 us)
Async XLA Ops:
  1.4 27.7 %all-to-all-start = ((bf16[32,16,128]{2,1,0:T(8,128)(2,1)}), bf16[32,16,128]{2,1,0:T(8,128)(2,1)S(1)}, u32[]{:S(2)}, u32[]{:S(2)}) async-start(bf16[32,16,128]{2,1,0:T(8,128)(2,1)} %broadcast_in_dim.8), calls=%async_computation | async-start | bytes 262144 | tf_op jit(solution)/shard_map/all_to_all | solution.py:196
  29.1 1.4 %copy-start = (bf16[1,2,3072,128]{3,2,1,0:T(8,128)(2,1)S(1)}, bf16[1,2,3072,128]{3,2,1,0:T(8,128)(2,1)}, u32[]{:S(2)}) copy-start(bf16[1,2,3072,128]{3,2,1,0:T(8,128)(2,1)} %param.9) | copy-start | bytes 4718596
  30.5 1.4 %copy-start.1 = (bf16[1,2,3072,128]{3,2,1,0:T(8,128)(2,1)S(1)}, bf16[1,2,3072,128]{3,2,1,0:T(8,128)(2,1)}, u32[]{:S(2)}) copy-start(bf16[1,2,3072,128]{3,2,1,0:T(8,128)(2,1)} %param.10) | copy-start | bytes 4718596
  31.9 0.7 copy-start.2
  32.6 0.7 copy-start.3
  33.3 0.7 copy-start.4
  72.4 14.2 %all-to-all-start.3 = ((bf16[16,128,128]{2,1,0:T(8,128)(2,1)}), bf16[16,128,128]{2,1,0:T(8,128)(2,1)S(1)}, u32[]{:S(2)}, u32[]{:S(2)}) async-start(bf16[16,128,128]{2,1,0:T(8,128)(2,1)} %combine_last.1), calls=%async_computation.3 | async-start | bytes 1048576 | tf_op jit(solution)/shard_map/all_to_all | solution.py:203
  86.7 0.8 copy-start.5

commit v2 on v1

--- a/solution.py
+++ b/solution.py
@@ -12,7 +12,8 @@
 NEW = 16
 QPK = 16
 NEG = -1e30
-CTX = ("x", "zl")
+Z = ("za", "zb")
+CTX = ("x",) + Z
 HEAD = ("zh", "core")
 BF = jnp.bfloat16
 F32 = jnp.float32
@@ -100,48 +101,78 @@
 def combine_kernel(r_ref, out_ref, *, rate, last):
     sources = r_ref.shape[0]
     copies = out_ref.shape[0]
-    stats = [unpack_stats(r_ref[s, 128:, :]) for s in range(sources)]
+    rows = r_ref.shape[1] - STAT_ROWS
+    size = r_ref.shape[2]
+    stats = [unpack_stats(r_ref[s, rows:, :]) for s in range(sources)]
     top = functools.reduce(jnp.maximum, [m for m, _ in stats])
     weights = [t * jnp.exp2((m - top) * rate) for m, t in stats]
     total = functools.reduce(jnp.add, weights)
-    at = iota((128, 128), 0)
-    factors = jnp.zeros((128, 128), F32)
+    at = iota((size, size), 0)
+    factors = jnp.zeros((size, size), F32)
     for s in range(sources):
         factors = jnp.where(at == s, weights[s] / total, factors)
     factors = jnp.transpose(factors)
-    out = jnp.zeros((128, 128), F32)
+    out = jnp.zeros((rows, size), F32)
     for s in range(sources):
-        out = out + factors[:, s : s + 1] * r_ref[s, 0:128, :].astype(F32)
+        out = out + factors[0:rows, s : s + 1] * r_ref[s, 0:rows, :].astype(F32)
     out = out.astype(BF)
-    for c in range(copies):
-        out_ref[c, 0:128, :] = out
-    if not last:
+    if last:
+        for c in range(copies):
+            out_ref[c] = out
+        return
+    half = rows // 2
+    for h in range(2):
+        if h:
+            top, total = (jnp.concatenate([v[:, half:], v[:, :half]], axis=1) for v in (top, total))
         tail = pack_stats(top, total)
-        for c in range(copies):
-            out_ref[c, 128:, :] = tail
+        for c in range(h, copies, 2):
+            out_ref[c, 0:half, :] = out[h * half : (h + 1) * half]
+            out_ref[c, half:, :] = tail
 
 
 def project_kernel(r_ref, w_ref, out_ref):
-    n_x, n_y, rows, size = r_ref.shape
+    n_x, n_y, n_z, rows, size = r_ref.shape
     per = rows // NEW
     acc = jnp.zeros((n_y * NEW, w_ref.shape[1]), F32)
     for x in range(n_x):
-        for j in range(0, per, 2):
-            block = jnp.concatenate(
-                [
-                    jnp.concatenate([r_ref[x, y, pl.ds((j + i) * NEW, NEW), :] for y in range(n_y)], axis=0)
-                    for i in range(2)
-                ],
-                axis=1,
-            )
-            acc = acc + jnp.dot(
-                block, w_ref[pl.ds((x * per + j) * size, 2 * size), :], preferred_element_type=F32
-            )
+        for z in range(n_z):
+            for j in range(0, per, 2):
+                block = jnp.concatenate(
+                    [
+                        jnp.concatenate([r_ref[x, y, z, pl.ds((j + i) * NEW, NEW), :] for y in range(n_y)], axis=0)
+                        for i in range(2)
+                    ],
+                    axis=1,
+                )
+                start = ((x * n_z + z) * per + j) * size
+                acc = acc + jnp.dot(block, w_ref[pl.ds(start, 2 * size), :], preferred_element_type=F32)
     out_ref[...] = acc.astype(BF).reshape(out_ref.shape)
 
 
 def in_vmem(n):
     return [pl.BlockSpec(memory_space=pltpu.VMEM)] * n
+
+
+def stage_kernel(*refs):
+    count = (len(refs) - 1) // 2
+    copies = [pltpu.make_async_copy(refs[n], refs[count + n], refs[-1].at[n]) for n in range(count)]
+    for copy in copies:
+        copy.start()
+    for copy in copies:
+        copy.wait()
+
+
+def stage(*arrays):
+    return pl.pallas_call(
+        stage_kernel,
+        out_shape=[jax.ShapeDtypeStruct(a.shape, a.dtype) for a in arrays],
+        in_specs=[pl.BlockSpec(memory_space=pltpu.HBM)] * len(arrays),
+        out_specs=in_vmem(len(arrays)),
+        scratch_shapes=[pltpu.SemaphoreType.DMA((len(arrays),))],
+        compiler_params=pltpu.CompilerParams(vmem_limit_bytes=8 << 20),
+        cost_estimate=pl.CostEstimate(flops=0, bytes_accessed=2 * sum(a.size * 2 for a in arrays), transcendentals=0),
+        name="stage",
+    )(*[pltpu.with_memory_space_constraint(a, pltpu.HBM) for a in arrays])
 
 
 def attend(info, q, keys, values, fresh_keys, fresh_values, pos):
@@ -155,7 +186,7 @@
         in_specs=[pl.BlockSpec(memory_space=pltpu.SMEM)] + in_vmem(6),
         out_specs=pl.BlockSpec(memory_space=pltpu.VMEM),
         scratch_shapes=[pltpu.VMEM((NEW * QPK, slots), F32)],
-        compiler_params=pltpu.CompilerParams(vmem_limit_bytes=24 << 20),
+        compiler_params=pltpu.CompilerParams(vmem_limit_bytes=16 << 20),
         cost_estimate=pl.CostEstimate(
             flops=flops, bytes_accessed=2 * heads * slots * size * 2, transcendentals=heads * NEW * QPK * slots
         ),
@@ -164,12 +195,13 @@
 
 
 def combine(r, copies, last, rate):
-    rows = 128 if last else 128 + STAT_ROWS
+    rows = r.shape[1] - STAT_ROWS if last else (r.shape[1] - STAT_ROWS) // 2 + STAT_ROWS
     return pl.pallas_call(
         functools.partial(combine_kernel, rate=rate, last=last),
         out_shape=jax.ShapeDtypeStruct((copies, rows, r.shape[2]), BF),
         in_specs=in_vmem(1),
         out_specs=pl.BlockSpec(memory_space=pltpu.VMEM),
+        compiler_params=pltpu.CompilerParams(vmem_limit_bytes=8 << 20),
         name="combine_last" if last else "combine",
     )(r)
 
@@ -180,6 +212,7 @@
         out_shape=jax.ShapeDtypeStruct((r.shape[1], NEW, w.shape[1]), BF),
         in_specs=in_vmem(2),
         out_specs=pl.BlockSpec(memory_space=pltpu.VMEM),
+        compiler_params=pltpu.CompilerParams(vmem_limit_bytes=8 << 20),
         name="project",
     )(r, w)
 
@@ -194,21 +227,25 @@
     mine = queries[0].reshape(1, -1, size)
     sent = jnp.broadcast_to(mine, (n_ctx,) + mine.shape[1:])
     q = lax.all_to_all(sent, CTX, 0, 0, tiled=True)
-    part = attend(info, q, cache_keys[0], cache_values[0], new_keys[0], new_values[0], positions)
+    keys, values, fresh_keys, fresh_values, pos = stage(
+        cache_keys[0], cache_values[0], new_keys[0], new_values[0], positions
+    )
+    part = attend(info, q, keys, values, fresh_keys, fresh_values, pos)
     part = lax.all_to_all(part, "x", 0, 0, tiled=True)
-    part = combine(part, lax.axis_size("zl"), False, rate)
-    part = lax.all_to_all(part, "zl", 0, 0, tiled=True)
-    n_x, n_y = lax.axis_size("x"), lax.axis_size("y")
-    rows = combine(part, n_x * n_y, True, rate)
-    rows = lax.all_to_all(rows, ("x", "y"), 0, 0, tiled=True)
-    out = project(rows.reshape(n_x, n_y, *rows.shape[1:]), out_weight)
+    part = combine(part, lax.axis_size(Z), False, rate)
+    part = lax.all_to_all(part, Z, 0, 0, tiled=True)
+    spread = ("x", "y", "zb")
+    sizes = tuple(lax.axis_size(a) for a in spread)
+    rows = combine(part, math.prod(sizes), True, rate)
+    rows = lax.all_to_all(rows, spread, 0, 0, tiled=True)
+    out = project(rows.reshape(*sizes, *rows.shape[1:]), out_weight)
     every = lax.all_gather(out, HEAD, axis=0)
     mine = lax.dynamic_index_in_dim(every, lax.axis_index(HEAD), 1, keepdims=True)
     return jnp.sum(mine.astype(F32), axis=0).astype(BF)
 
 
 def solution(mesh):
-    fine = Mesh(mesh.devices.reshape(4, 8, 2, 2, 4), ("x", "zl", "zh", "core", "y"))
+    fine = Mesh(mesh.devices.reshape(4, 4, 2, 2, 2, 4), ("x", "za", "zb", "zh", "core", "y"))
     in_specs = (
         P("y", HEAD, CTX, None),
         P("y", HEAD, CTX, None),

time: 110 us -> 94.4 us (0.86)
  blocking collectives: 49.2 us -> 43.3 us
  local copies, waits for them, and re-layouts: 7.01 us -> 1.35 us
  Pallas kernels: 10.5 us -> 7.77 us
  waiting for transfers between devices: 20.1 us -> 18.8 us
    all_to_all x1, blocking collectives: 22.4 us -> 16.4 us  [body(): part = lax.all_to_all(part, Z, 0, 0, tiled=True)]
    unnamed x12 -> x2, local copies, waits for them, and re-layouts: 5.65 us -> 0.01 us
    pallas_call x2, Pallas kernels: 4.07 us -> 1.41 us  [combine(): pl.pallas_call(functools.partial(combine_kernel, rate=rate, last=last), o...]
    pallas_call x1, Pallas kernels: 2.31 us -> 0.33 us  [project(): pl.pallas_call(project_kernel, out_shape=jax.ShapeDtypeStruct((r.shape[1]...]
    all_to_all x1, waiting for transfers between devices: 11 us -> 9.1 us  [body(): q = lax.all_to_all(sent, CTX, 0, 0, tiled=True)]
    pallas_call x0 -> x1, Pallas kernels: none -> 1.94 us  [stage(): pl.pallas_call(stage_kernel, out_shape=[jax.ShapeDtypeStruct(a.shape, a.d...]
  transfers between devices with their start and end apart: 2 -> 2, of which waited for: 2 -> 2; matrix products, arithmetic and copies ran while one was open for 0% -> 0% of each run, Pallas kernels for 0% -> 2%
where the time goes in v2:
time: 94.4 us; the launch traced here: 94 us
  blocking collectives  43.3 us (46%)
  starting transfers between devices  21.4 us (23%)
  waiting for transfers between devices  18.8 us (20%)
  Pallas kernels  7.77 us (8%)
  local copies, waits for them, and re-layouts  1.35 us (1%)
    all_gather x1, blocking collectives, body(): every = lax.all_gather(out, HEAD, axis=0)  19.5 us
    all_to_all x1, blocking collectives, body(): part = lax.all_to_all(part, Z, 0, 0, tiled=True)  16.4 us
    all_to_all x1, starting transfers between devices, body(): q = lax.all_to_all(sent, CTX, 0, 0, tiled=True)  15.9 us
    all_to_all x1, waiting for transfers between devices, body(): rows = lax.all_to_all(rows, spread, 0, 0, tiled=True)  9.73 us
    all_to_all x1, waiting for transfers between devices, body(): q = lax.all_to_all(sent, CTX, 0, 0, tiled=True)  9.1 us
    all_to_all x1, blocking collectives, body(): part = lax.all_to_all(part, 'x', 0, 0, tiled=True)  7.4 us
    all_to_all x1, starting transfers between devices, body(): rows = lax.all_to_all(rows, spread, 0, 0, tiled=True)  5.47 us
    pallas_call x1, Pallas kernels, attend(): pl.pallas_call(functools.partial(attend_kernel, rate=rate, chunk=chunk),...  4.1 us
  transfers between devices with their start and end apart: 2, of which 2 were waited for; matrix products, arithmetic and copies ran while one was open for 0% of the time, Pallas kernels for 2%

profile of v2, /device:TPU:1, one launch (start us, length us, event | category | flops | bytes accessed | tf_op | source)
XLA Modules:
  0.0 94.0 jit_solution(8156987290159668634)
XLA Ops:
  0.0 1.3 %broadcast_in_dim.8 = bf16[32,16,128]{2,1,0:T(8,128)(2,1)} broadcast(bf16[16,128]{1,0:T(8,128)(2,1)} %bitcast.18), dimensions={1,2} | broadcast | bytes 135168 | tf_op jit(solution)/shard_map/broadcast_in_dim | solution.py:228
  1.3 15.9 %all-to-all-start = ((bf16[32,16,128]{2,1,0:T(8,128)(2,1)}), bf16[32,16,128]{2,1,0:T(8,128)(2,1)S(1)}, u32[]{:S(2)}, u32[]{:S(2)}) async-start(bf16[32,16,128]{2,1,0:T(8,128)(2,1)} %broadcast_in_dim.8), calls=%async_computation | async-start | bytes 262144 | tf_op jit(solution)/shard_map/all_to_all | solution.py:229
  17.9 1.9 %stage.1 = (bf16[2,3072,128]{2,1,0:T(8,128)(2,1)S(1)}, bf16[2,3072,128]{2,1,0:T(8,128)(2,1)S(1)}, bf16[2,16,128]{2,1,0:T(8,128)(2,1)S(1)}, bf16[2,16,128]{2,1,0:T(8,128)(2,1)S(1)}, s32[1,16]{1,0:T(1,128)S(1)}) custom-call(bf16[2,3072,128]{2,1,0:T(8,128)(2,1)} %bitcast.13, bf16[2,3072,128]{2,1,0:T(8,128)(2,1)} %bitcast.14, bf16[2,16,128]{2,1,0:T(8,128)(2,1)} %bitcast.16, ...), custom_call_target="tpu_custom_call" | custom-call | bytes 6324288 | tf_op jit(solution)/shard_map/stage/pallas_call | solution.py:166
  19.9 0.1 pad_add_fusion.info
  20.0 9.1 %all-to-all-done.q_ref = bf16[32,16,128]{2,1,0:T(8,128)(2,1)S(1)} async-done(((bf16[32,16,128]{2,1,0:T(8,128)(2,1)}), bf16[32,16,128]{2,1,0:T(8,128)(2,1)S(1)}, u32[]{:S(2)}, u32[]{:S(2)}) %all-to-all-start) | async-done | bytes 131104 | tf_op jit(solution)/shard_map/all_to_all | solution.py:229
  29.1 4.1 %attend.1 = bf16[4,144,128]{2,1,0:T(8,128)(2,1)S(1)} custom-call(s32[2]{0:T(128)S(1)} %pad_add_fusion.info, bf16[32,16,128]{2,1,0:T(8,128)(2,1)S(1)} %all-to-all-done.q_ref, bf16[2,3072,128]{2,1,0:T(8,128)(2,1)S(1)} %get-tuple-element.10.keys, bf16[2,3072,128]{2,1,0:T(8,128)(2,1)S(1)} %get-tuple-element.11.values, ...), custom_call_target="tpu_custom_call" | custom-call | flops 805306368 | bytes 3145728 | tf_op jit(solution)/shard_map/attend/pallas_call | solution.py:183
  33.2 0.0 copy-start
  33.2 7.4 %all_to_all.20.r_ref = bf16[4,144,128]{2,1,0:T(8,128)(2,1)S(1)} all-to-all(bf16[4,144,128]{2,1,0:T(8,128)(2,1)S(1)} %attend.1), channel_id=1, replica_groups=mesh['x'=4,'za'=4,'zb'=2,'zh'=2,'core'=2,'y'=4] {'x'}, dimensions={0} | all-to-all | bytes 294912 | tf_op jit(solution)/shard_map/all_to_all | solution.py:234
  40.6 0.3 combine.1
  40.9 16.4 %all_to_all.21.r_ref = bf16[8,80,128]{2,1,0:T(8,128)(2,1)S(1)} all-to-all(bf16[8,80,128]{2,1,0:T(8,128)(2,1)S(1)} %combine.1), channel_id=1, replica_groups=mesh['x'=4,'za'=4,'zb'=2,'zh'=2,'core'=2,'y'=4] {'za','zb'}, dimensions={0} | all-to-all | bytes 327680 | tf_op jit(solution)/shard_map/all_to_all | solution.py:236
  57.3 1.1 %combine_last.1 = bf16[32,64,128]{2,1,0:T(8,128)(2,1)} custom-call(bf16[8,80,128]{2,1,0:T(8,128)(2,1)S(1)} %all_to_all.21.r_ref), custom_call_target="tpu_custom_call" | custom-call | tf_op jit(solution)/shard_map/combine_last/pallas_call | solution.py:199
  58.4 5.5 %all-to-all-start.3 = ((bf16[32,64,128]{2,1,0:T(8,128)(2,1)}), bf16[32,64,128]{2,1,0:T(8,128)(2,1)S(1)}, u32[]{:S(2)}, u32[]{:S(2)}) async-start(bf16[32,64,128]{2,1,0:T(8,128)(2,1)} %combine_last.1), calls=%async_computation.3 | async-start | bytes 1048576 | tf_op jit(solution)/shard_map/all_to_all | solution.py:240
  63.9 9.7 %all-to-all-done.3 = bf16[32,64,128]{2,1,0:T(8,128)(2,1)S(1)} async-done(((bf16[32,64,128]{2,1,0:T(8,128)(2,1)}), bf16[32,64,128]{2,1,0:T(8,128)(2,1)S(1)}, u32[]{:S(2)}, u32[]{:S(2)}) %all-to-all-start.3) | async-done | bytes 524320 | tf_op jit(solution)/shard_map/all_to_all | solution.py:240
  73.6 0.0 copy-done
  73.6 0.3 project.1
  74.0 19.5 %all-gather = bf16[16,16,128]{2,1,0:T(8,128)(2,1)S(1)} all-gather(bf16[4,16,128]{2,1,0:T(8,128)(2,1)S(1)} %project.1), channel_id=2, replica_groups=mesh['x'=4,'za'=4,'zb'=2,'zh'=2,'core'=2,'y'=4] {'zh','core'}, dimensions={0}, use_global_device_ids=true | all-gather | bytes 81920 | tf_op jit(solution)/shard_map/all_gather | solution.py:242
  93.4 0.6 dynamic-slice_reduce_fusion
Async XLA Ops:
  1.3 27.7 %all-to-all-start = ((bf16[32,16,128]{2,1,0:T(8,128)(2,1)}), bf16[32,16,128]{2,1,0:T(8,128)(2,1)S(1)}, u32[]{:S(2)}, u32[]{:S(2)}) async-start(bf16[32,16,128]{2,1,0:T(8,128)(2,1)} %broadcast_in_dim.8), calls=%async_computation | async-start | bytes 262144 | tf_op jit(solution)/shard_map/all_to_all | solution.py:229
  33.2 40.5 %copy-start = (bf16[4096,128]{1,0:T(8,128)(2,1)S(1)}, bf16[4096,128]{1,0:T(8,128)(2,1)}, u32[]{:S(2)}) copy-start(bf16[4096,128]{1,0:T(8,128)(2,1)} %w_ref.1) | copy-start | bytes 3145732
  58.4 15.2 %all-to-all-start.3 = ((bf16[32,64,128]{2,1,0:T(8,128)(2,1)}), bf16[32,64,128]{2,1,0:T(8,128)(2,1)S(1)}, u32[]{:S(2)}, u32[]{:S(2)}) async-start(bf16[32,64,128]{2,1,0:T(8,128)(2,1)} %combine_last.1), calls=%async_computation.3 | async-start | bytes 1048576 | tf_op jit(solution)/shard_map/all_to_all | solution.py:240

commit v3 on v2

--- a/solution.py
+++ b/solution.py
@@ -53,40 +53,25 @@
 
 def attend_kernel(info, q_ref, keys, values, fresh_keys, fresh_values, pos_ref, out_ref, scores, *, rate, chunk):
     heads, slots, size = keys.shape
-    n_rows = heads * NEW * QPK
     rows = NEW * QPK
     valid = info[0]
     fresh_on = info[1]
-    queries = q_ref[...].reshape(n_rows, size)
-    dest = iota((n_rows, 1), 0)
-    head, j, token = dest // rows, (dest // NEW) % QPK, dest % NEW
     half_rows = QPK // 2
-    source = (token * 2 + j // half_rows) * (heads * half_rows) + head * half_rows + j % half_rows
-    order = jnp.where(iota((n_rows, n_rows), 1) == source, 1.0, 0.0).astype(BF)
-    queries = jnp.dot(order, queries, preferred_element_type=F32).astype(BF)
+    n = NEW * half_rows
+    dest = iota((n, 1), 0)
+    order = jnp.where(iota((n, n), 1) == dest % NEW * half_rows + dest // NEW, 1.0, 0.0).astype(BF)
+    arrived = q_ref[...].astype(F32).reshape(NEW, 2, heads * half_rows, size)
+
+    def ordered(k, h):
+        block = arrived[:, h, k * half_rows : (k + 1) * half_rows, :].reshape(n, size).astype(BF)
+        return jnp.dot(order, block, preferred_element_type=F32).astype(BF)
+
 
     pos = jnp.broadcast_to(pos_ref[...], (rows, NEW))
     mine = jnp.where(iota((rows, NEW), 0) % NEW == iota((rows, NEW), 1), pos, 0)
     allow = jnp.logical_and(pos <= jnp.sum(mine, axis=1, keepdims=True), fresh_on > 0)
 
-    for k in range(heads):
-        q = queries[k * rows : (k + 1) * rows]
-        fresh = jnp.where(allow, dot_nt(q, fresh_keys[k]), NEG)
-        part = jnp.full((rows, 128), NEG, F32)
-        for c in range(slots // chunk):
-            s = dot_nt(q, keys[k, pl.ds(c * chunk, chunk), :])
-            s = jnp.where(iota((1, chunk), 1) + c * chunk < valid, s, NEG)
-            scores[:, pl.ds(c * chunk, chunk)] = s
-            for i in range(chunk // 128):
-                part = jnp.maximum(part, s[:, i * 128 : (i + 1) * 128])
-        top = jnp.maximum(jnp.max(part, axis=1, keepdims=True), jnp.max(fresh, axis=1, keepdims=True))
-        weights = jnp.exp2((fresh - top) * rate).astype(BF)
-        fresh_ones = jnp.concatenate([fresh_values[k], jnp.ones((NEW, size), BF)], axis=1)
-        acc = jnp.dot(weights, fresh_ones, preferred_element_type=F32)
-        for c in range(slots // chunk):
-            w = jnp.exp2((scores[:, pl.ds(c * chunk, chunk)] - top) * rate).astype(BF)
-            v = jnp.concatenate([values[k, pl.ds(c * chunk, chunk), :], jnp.ones((chunk, size), BF)], axis=1)
-            acc = acc + jnp.dot(w, v, preferred_element_type=F32)
+    def finish(k, acc, top):
         total = acc[:, size:]
         attended = (acc[:, :size] / total).astype(BF)
         for h in range(2):
@@ -96,6 +81,30 @@
             stats = jnp.transpose(cols)
             out_ref[2 * k + h, 0:128, :] = attended[part_rows]
             out_ref[2 * k + h, 128:, :] = pack_stats(stats[0:1], stats[1:2])
+
+    tops = []
+    for k in range(heads):
+        q = jnp.concatenate([ordered(k, 0), ordered(k, 1)], axis=0)
+        fresh = jnp.where(allow, dot_nt(q, fresh_keys[k]), NEG)
+        part = jnp.full((rows, 128), NEG, F32)
+        for c in range(slots // chunk):
+            s = dot_nt(q, keys[k, pl.ds(c * chunk, chunk), :])
+            s = jnp.where(iota((1, chunk), 1) + c * chunk < valid, s, NEG)
+            scores[k, :, pl.ds(c * chunk, chunk)] = s
+            for i in range(chunk // 128):
+                part = jnp.maximum(part, s[:, i * 128 : (i + 1) * 128])
+        top = jnp.maximum(jnp.max(part, axis=1, keepdims=True), jnp.max(fresh, axis=1, keepdims=True))
+        tops.append((top, fresh))
+    for k in range(heads):
+        top, fresh = tops[k]
+        weights = jnp.exp2((fresh - top) * rate).astype(BF)
+        fresh_ones = jnp.concatenate([fresh_values[k], jnp.ones((NEW, size), BF)], axis=1)
+        acc = jnp.dot(weights, fresh_ones, preferred_element_type=F32)
+        for c in range(slots // chunk):
+            w = jnp.exp2((scores[k, :, pl.ds(c * chunk, chunk)] - top) * rate).astype(BF)
+            v = jnp.concatenate([values[k, pl.ds(c * chunk, chunk), :], jnp.ones((chunk, size), BF)], axis=1)
+            acc = acc + jnp.dot(w, v, preferred_element_type=F32)
+        finish(k, acc, top)
 
 
 def combine_kernel(r_ref, out_ref, *, rate, last):
@@ -178,15 +187,15 @@
 def attend(info, q, keys, values, fresh_keys, fresh_values, pos):
     heads, slots, size = keys.shape
     rate = math.log2(math.e) / size**0.5
-    chunk = min(slots, 512)
+    chunk = min(slots, 256)
     flops = 4 * heads * NEW * QPK * slots * size
     return pl.pallas_call(
         functools.partial(attend_kernel, rate=rate, chunk=chunk),
         out_shape=jax.ShapeDtypeStruct((2 * heads, 128 + STAT_ROWS, size), BF),
         in_specs=[pl.BlockSpec(memory_space=pltpu.SMEM)] + in_vmem(6),
         out_specs=pl.BlockSpec(memory_space=pltpu.VMEM),
-        scratch_shapes=[pltpu.VMEM((NEW * QPK, slots), F32)],
-        compiler_params=pltpu.CompilerParams(vmem_limit_bytes=16 << 20),
+        scratch_shapes=[pltpu.VMEM((heads, NEW * QPK, slots), F32)],
+        compiler_params=pltpu.CompilerParams(vmem_limit_bytes=13 << 20),
         cost_estimate=pl.CostEstimate(
             flops=flops, bytes_accessed=2 * heads * slots * size * 2, transcendentals=heads * NEW * QPK * slots
         ),
@@ -215,6 +224,25 @@
         compiler_params=pltpu.CompilerParams(vmem_limit_bytes=8 << 20),
         name="project",
     )(r, w)
+
+
+def total_kernel(every, out_ref):
+    mine = lax.axis_index(HEAD)
+    total = every[0, mine].astype(F32)
+    for h in range(1, every.shape[0]):
+        total = total + every[h, mine].astype(F32)
+    out_ref[0] = total.astype(BF)
+
+
+def total_of(every):
+    return pl.pallas_call(
+        total_kernel,
+        out_shape=jax.ShapeDtypeStruct((1,) + every.shape[2:], BF),
+        in_specs=in_vmem(1),
+        out_specs=pl.BlockSpec(memory_space=pltpu.VMEM),
+        compiler_params=pltpu.CompilerParams(vmem_limit_bytes=2 << 20),
+        name="total",
+    )(every)
 
 
 def body(queries, cache_keys, cache_values, new_keys, new_values, lengths, positions, out_weight):
@@ -227,10 +255,8 @@
     mine = queries[0].reshape(1, -1, size)
     sent = jnp.broadcast_to(mine, (n_ctx,) + mine.shape[1:])
     q = lax.all_to_all(sent, CTX, 0, 0, tiled=True)
-    keys, values, fresh_keys, fresh_values, pos = stage(
-        cache_keys[0], cache_values[0], new_keys[0], new_values[0], positions
-    )
-    part = attend(info, q, keys, values, fresh_keys, fresh_values, pos)
+    staged = stage(cache_keys[0], cache_values[0], new_keys[0], new_values[0], positions)
+    part = attend(info, q, *staged)
     part = lax.all_to_all(part, "x", 0, 0, tiled=True)
     part = combine(part, lax.axis_size(Z), False, rate)
     part = lax.all_to_all(part, Z, 0, 0, tiled=True)
@@ -240,8 +266,7 @@
     rows = lax.all_to_all(rows, spread, 0, 0, tiled=True)
     out = project(rows.reshape(*sizes, *rows.shape[1:]), out_weight)
     every = lax.all_gather(out, HEAD, axis=0)
-    mine = lax.dynamic_index_in_dim(every, lax.axis_index(HEAD), 1, keepdims=True)
-    return jnp.sum(mine.astype(F32), axis=0).astype(BF)
+    return total_of(every)
 
 
 def solution(mesh):

time: 94.4 us -> 92.4 us (0.979)
  blocking collectives: 43.3 us -> 58.3 us
  waiting for transfers between devices: 18.8 us -> 9.1 us
  starting transfers between devices: 21.4 us -> 15.9 us
  Pallas kernels: 7.77 us -> 6.65 us
    all_to_all x0 -> x1, blocking collectives: none -> 15 us  [body(): rows = lax.all_to_all(rows, spread, 0, 0, tiled=True)]
    all_to_all x1 -> x0, waiting for transfers between devices: 9.73 us -> none  [body(): rows = lax.all_to_all(rows, spread, 0, 0, tiled=True)]
    all_to_all x1 -> x0, starting transfers between devices: 5.47 us -> none  [body(): rows = lax.all_to_all(rows, spread, 0, 0, tiled=True)]
  transfers between devices with their start and end apart: 2 -> 1, of which waited for: 2 -> 1; matrix products, arithmetic and copies ran while one was open for 0% -> 0% of each run, Pallas kernels for 2% -> 2%
where the time goes in v3:
time: 92.4 us; the launch traced here: 92.1 us
  blocking collectives  58.3 us (63%)
  starting transfers between devices  15.9 us (17%)
  waiting for transfers between devices  9.1 us (10%)
  Pallas kernels  6.65 us (7%)
  local copies, waits for them, and re-layouts  1.35 us (1%)
    all_gather x1, blocking collectives, body(): every = lax.all_gather(out, HEAD, axis=0)  19.5 us
    all_to_all x1, blocking collectives, body(): part = lax.all_to_all(part, Z, 0, 0, tiled=True)  16.4 us
    all_to_all x1, starting transfers between devices, body(): q = lax.all_to_all(sent, CTX, 0, 0, tiled=True)  15.9 us
    all_to_all x1, blocking collectives, body(): rows = lax.all_to_all(rows, spread, 0, 0, tiled=True)  15 us
    all_to_all x1, waiting for transfers between devices, body(): q = lax.all_to_all(sent, CTX, 0, 0, tiled=True)  9.1 us
    all_to_all x1, blocking collectives, body(): part = lax.all_to_all(part, 'x', 0, 0, tiled=True)  7.4 us
    pallas_call x1, Pallas kernels, attend(): pl.pallas_call(functools.partial(attend_kernel, rate=rate, chunk=chunk),...  3.18 us
    pallas_call x1, Pallas kernels, stage(): pl.pallas_call(stage_kernel, out_shape=[jax.ShapeDtypeStruct(a.shape, a.d...  1.94 us
  transfers between devices with their start and end apart: 1, of which 1 were waited for; matrix products, arithmetic and copies ran while one was open for 0% of the time, Pallas kernels for 2%

profile of v3, /device:TPU:1, one launch (start us, length us, event | category | flops | bytes accessed | tf_op | source)
XLA Modules:
  0.0 92.1 jit_solution(5058257526080725576)
XLA Ops:
  0.0 1.3 %broadcast_in_dim.8 = bf16[32,16,128]{2,1,0:T(8,128)(2,1)} broadcast(bf16[16,128]{1,0:T(8,128)(2,1)} %bitcast.17), dimensions={1,2} | broadcast | bytes 135168 | tf_op jit(solution)/shard_map/broadcast_in_dim | solution.py:256
  1.3 15.9 %all-to-all-start = ((bf16[32,16,128]{2,1,0:T(8,128)(2,1)}), bf16[32,16,128]{2,1,0:T(8,128)(2,1)S(1)}, u32[]{:S(2)}, u32[]{:S(2)}) async-start(bf16[32,16,128]{2,1,0:T(8,128)(2,1)} %broadcast_in_dim.8), calls=%async_computation | async-start | bytes 262144 | tf_op jit(solution)/shard_map/all_to_all | solution.py:257
  17.9 1.9 %stage.1 = (bf16[2,3072,128]{2,1,0:T(8,128)(2,1)S(1)}, bf16[2,3072,128]{2,1,0:T(8,128)(2,1)S(1)}, bf16[2,16,128]{2,1,0:T(8,128)(2,1)S(1)}, bf16[2,16,128]{2,1,0:T(8,128)(2,1)S(1)}, s32[1,16]{1,0:T(1,128)S(1)}) custom-call(bf16[2,3072,128]{2,1,0:T(8,128)(2,1)} %bitcast.13, bf16[2,3072,128]{2,1,0:T(8,128)(2,1)} %bitcast.14, bf16[2,16,128]{2,1,0:T(8,128)(2,1)} %bitcast.15, ...), custom_call_target="tpu_custom_call" | custom-call | bytes 6324288 | tf_op jit(solution)/shard_map/stage/pallas_call | solution.py:175
  19.9 0.1 pad_add_fusion.info
  20.0 9.1 %all-to-all-done.q_ref = bf16[32,16,128]{2,1,0:T(8,128)(2,1)S(1)} async-done(((bf16[32,16,128]{2,1,0:T(8,128)(2,1)}), bf16[32,16,128]{2,1,0:T(8,128)(2,1)S(1)}, u32[]{:S(2)}, u32[]{:S(2)}) %all-to-all-start) | async-done | bytes 131104 | tf_op jit(solution)/shard_map/all_to_all | solution.py:257
  29.1 3.2 %attend.1 = bf16[4,144,128]{2,1,0:T(8,128)(2,1)S(1)} custom-call(s32[2]{0:T(128)S(1)} %pad_add_fusion.info, bf16[32,16,128]{2,1,0:T(8,128)(2,1)S(1)} %all-to-all-done.q_ref, bf16[2,3072,128]{2,1,0:T(8,128)(2,1)S(1)} %get-tuple-element.10.keys, bf16[2,3072,128]{2,1,0:T(8,128)(2,1)S(1)} %get-tuple-element.11.values, ...), custom_call_target="tpu_custom_call" | custom-call | flops 805306368 | bytes 3145728 | tf_op jit(solution)/shard_map/attend/pallas_call | solution.py:192
  32.2 0.0 copy-start
  32.3 7.4 %all_to_all.20.r_ref = bf16[4,144,128]{2,1,0:T(8,128)(2,1)S(1)} all-to-all(bf16[4,144,128]{2,1,0:T(8,128)(2,1)S(1)} %attend.1), channel_id=1, replica_groups=mesh['x'=4,'za'=4,'zb'=2,'zh'=2,'core'=2,'y'=4] {'x'}, dimensions={0} | all-to-all | bytes 294912 | tf_op jit(solution)/shard_map/all_to_all | solution.py:260
  39.6 0.3 combine.1
  39.9 16.4 %all_to_all.21.r_ref = bf16[8,80,128]{2,1,0:T(8,128)(2,1)S(1)} all-to-all(bf16[8,80,128]{2,1,0:T(8,128)(2,1)S(1)} %combine.1), channel_id=1, replica_groups=mesh['x'=4,'za'=4,'zb'=2,'zh'=2,'core'=2,'y'=4] {'za','zb'}, dimensions={0} | all-to-all | bytes 327680 | tf_op jit(solution)/shard_map/all_to_all | solution.py:262
  56.4 0.3 combine_last.1
  56.7 15.0 %all_to_all.22 = bf16[32,64,128]{2,1,0:T(8,128)(2,1)S(1)} all-to-all(bf16[32,64,128]{2,1,0:T(8,128)(2,1)S(1)} %combine_last.1), channel_id=1, replica_groups=mesh['x'=4,'za'=4,'zb'=2,'zh'=2,'core'=2,'y'=4] {'x','y','zb'}, dimensions={0} | all-to-all | bytes 1048576 | tf_op jit(solution)/shard_map/all_to_all | solution.py:266
  71.7 0.0 copy-done
  71.7 0.3 project.1
  72.0 19.5 %all-gather = bf16[16,16,128]{2,1,0:T(8,128)(2,1)S(1)} all-gather(bf16[4,16,128]{2,1,0:T(8,128)(2,1)S(1)} %project.1), channel_id=2, replica_groups=mesh['x'=4,'za'=4,'zb'=2,'zh'=2,'core'=2,'y'=4] {'zh','core'}, dimensions={0}, use_global_device_ids=true | all-gather | bytes 81920 | tf_op jit(solution)/shard_map/all_gather | solution.py:268
  91.5 0.6 total.1
Async XLA Ops:
  1.3 27.7 %all-to-all-start = ((bf16[32,16,128]{2,1,0:T(8,128)(2,1)}), bf16[32,16,128]{2,1,0:T(8,128)(2,1)S(1)}, u32[]{:S(2)}, u32[]{:S(2)}) async-start(bf16[32,16,128]{2,1,0:T(8,128)(2,1)} %broadcast_in_dim.8), calls=%async_computation | async-start | bytes 262144 | tf_op jit(solution)/shard_map/all_to_all | solution.py:257
  32.2 39.5 %copy-start = (bf16[4096,128]{1,0:T(8,128)(2,1)S(1)}, bf16[4096,128]{1,0:T(8,128)(2,1)}, u32[]{:S(2)}) copy-start(bf16[4096,128]{1,0:T(8,128)(2,1)} %w_ref.1) | copy-start | bytes 3145732

commit v4 on v3

--- a/solution.py
+++ b/solution.py
@@ -51,25 +51,29 @@
     return top, total
 
 
-def attend_kernel(info, q_ref, keys, values, fresh_keys, fresh_values, pos_ref, out_ref, scores, *, rate, chunk):
+def attend_kernel(length, q_ref, keys, values, fresh_keys, fresh_values, pos_ref, out_ref, scores, *, rate, chunk):
     heads, slots, size = keys.shape
     rows = NEW * QPK
-    valid = info[0]
-    fresh_on = info[1]
+    here = lax.axis_index(CTX)
+    valid = length[0] - here * slots
     half_rows = QPK // 2
     n = NEW * half_rows
     dest = iota((n, 1), 0)
-    order = jnp.where(iota((n, n), 1) == dest % NEW * half_rows + dest // NEW, 1.0, 0.0).astype(BF)
-    arrived = q_ref[...].astype(F32).reshape(NEW, 2, heads * half_rows, size)
+    token = dest % NEW
+    n_x = lax.axis_size("x")
+    n_pairs = NEW // n_x
+    source = (token % n_pairs * n_x + token // n_pairs) * half_rows + dest // NEW
+    order = jnp.where(iota((n, n), 1) == source, 1.0, 0.0).astype(BF)
+    arrived = q_ref[...].astype(F32).reshape(n_pairs, 2, n_x, heads * half_rows, size)
 
     def ordered(k, h):
-        block = arrived[:, h, k * half_rows : (k + 1) * half_rows, :].reshape(n, size).astype(BF)
+        block = arrived[:, h, :, k * half_rows : (k + 1) * half_rows, :].reshape(n, size).astype(BF)
         return jnp.dot(order, block, preferred_element_type=F32).astype(BF)
 
 
     pos = jnp.broadcast_to(pos_ref[...], (rows, NEW))
     mine = jnp.where(iota((rows, NEW), 0) % NEW == iota((rows, NEW), 1), pos, 0)
-    allow = jnp.logical_and(pos <= jnp.sum(mine, axis=1, keepdims=True), fresh_on > 0)
+    allow = jnp.logical_and(pos <= jnp.sum(mine, axis=1, keepdims=True), here == 0)
 
     def finish(k, acc, top):
         total = acc[:, size:]
@@ -140,7 +144,7 @@
 
 
 def project_kernel(r_ref, w_ref, out_ref):
-    n_x, n_y, n_z, rows, size = r_ref.shape
+    n_z, n_x, n_y, rows, size = r_ref.shape
     per = rows // NEW
     acc = jnp.zeros((n_y * NEW, w_ref.shape[1]), F32)
     for x in range(n_x):
@@ -148,7 +152,7 @@
             for j in range(0, per, 2):
                 block = jnp.concatenate(
                     [
-                        jnp.concatenate([r_ref[x, y, z, pl.ds((j + i) * NEW, NEW), :] for y in range(n_y)], axis=0)
+                        jnp.concatenate([r_ref[z, x, y, pl.ds((j + i) * NEW, NEW), :] for y in range(n_y)], axis=0)
                         for i in range(2)
                     ],
                     axis=1,
@@ -184,7 +188,7 @@
     )(*[pltpu.with_memory_space_constraint(a, pltpu.HBM) for a in arrays])
 
 
-def attend(info, q, keys, values, fresh_keys, fresh_values, pos):
+def attend(length, q, keys, values, fresh_keys, fresh_values, pos):
     heads, slots, size = keys.shape
     rate = math.log2(math.e) / size**0.5
     chunk = min(slots, 256)
@@ -200,7 +204,7 @@
             flops=flops, bytes_accessed=2 * heads * slots * size * 2, transcendentals=heads * NEW * QPK * slots
         ),
         name="attend",
-    )(info, q, keys, values, fresh_keys, fresh_values, pos)
+    )(length, q, keys, values, fresh_keys, fresh_values, pos)
 
 
 def combine(r, copies, last, rate):
@@ -247,20 +251,17 @@
 
 def body(queries, cache_keys, cache_values, new_keys, new_values, lengths, positions, out_weight):
     size = cache_keys.shape[3]
-    slots = cache_keys.shape[2]
     rate = math.log2(math.e) / size**0.5
     n_ctx = lax.axis_size(CTX)
-    here = lax.axis_index(CTX)
-    info = jnp.stack([lengths[0] - here * slots, (here == 0).astype(jnp.int32)])
     mine = queries[0].reshape(1, -1, size)
     sent = jnp.broadcast_to(mine, (n_ctx,) + mine.shape[1:])
-    q = lax.all_to_all(sent, CTX, 0, 0, tiled=True)
+    q = lax.all_to_all(sent, Z + ("x",), 0, 0, tiled=True)
     staged = stage(cache_keys[0], cache_values[0], new_keys[0], new_values[0], positions)
-    part = attend(info, q, *staged)
+    part = attend(lengths, q, *staged)
     part = lax.all_to_all(part, "x", 0, 0, tiled=True)
     part = combine(part, lax.axis_size(Z), False, rate)
     part = lax.all_to_all(part, Z, 0, 0, tiled=True)
-    spread = ("x", "y", "zb")
+    spread = ("zb", "x", "y")
     sizes = tuple(lax.axis_size(a) for a in spread)
     rows = combine(part, math.prod(sizes), True, rate)
     rows = lax.all_to_all(rows, spread, 0, 0, tiled=True)

time: 92.4 us -> 90.3 us (0.977)
  blocking collectives: 58.3 us -> 56.3 us
    all_to_all x1, blocking collectives: 15 us -> 14 us  [body(): rows = lax.all_to_all(rows, spread, 0, 0, tiled=True)]
where the time goes in v4:
time: 90.3 us; the launch traced here: 90 us
  blocking collectives  56.3 us (62%)
  starting transfers between devices  15.9 us (18%)
  waiting for transfers between devices  9.54 us (11%)
  Pallas kernels  6.18 us (7%)
  local copies, waits for them, and re-layouts  1.35 us (1%)
    all_gather x1, blocking collectives, body(): every = lax.all_gather(out, HEAD, axis=0)  19.1 us
    all_to_all x1, starting transfers between devices, body(): q = lax.all_to_all(sent, Z + ('x',), 0, 0, tiled=True)  15.9 us
    all_to_all x1, blocking collectives, body(): part = lax.all_to_all(part, Z, 0, 0, tiled=True)  15.7 us
    all_to_all x1, blocking collectives, body(): rows = lax.all_to_all(rows, spread, 0, 0, tiled=True)  14 us
    all_to_all x1, waiting for transfers between devices, body(): q = lax.all_to_all(sent, Z + ('x',), 0, 0, tiled=True)  9.54 us
    all_to_all x1, blocking collectives, body(): part = lax.all_to_all(part, 'x', 0, 0, tiled=True)  7.51 us
    pallas_call x1, Pallas kernels, attend(): pl.pallas_call(functools.partial(attend_kernel, rate=rate, chunk=chunk),...  2.71 us
    pallas_call x1, Pallas kernels, stage(): pl.pallas_call(stage_kernel, out_shape=[jax.ShapeDtypeStruct(a.shape, a.d...  1.94 us
  transfers between devices with their start and end apart: 1, of which 1 were waited for; matrix products, arithmetic and copies ran while one was open for 0% of the time, Pallas kernels for 2%

profile of v4, /device:TPU:1, one launch (start us, length us, event | category | flops | bytes accessed | tf_op | source)
XLA Modules:
  0.0 90.0 jit_solution(9979390284920313094)
XLA Ops:
  0.0 1.3 %broadcast_in_dim.8 = bf16[32,16,128]{2,1,0:T(8,128)(2,1)} broadcast(bf16[16,128]{1,0:T(8,128)(2,1)} %bitcast.13), dimensions={1,2} | broadcast | bytes 135168 | tf_op jit(solution)/shard_map/broadcast_in_dim | solution.py:257
  1.3 15.9 %all-to-all-start = ((bf16[32,16,128]{2,1,0:T(8,128)(2,1)}), bf16[32,16,128]{2,1,0:T(8,128)(2,1)S(1)}, u32[]{:S(2)}, u32[]{:S(2)}) async-start(bf16[32,16,128]{2,1,0:T(8,128)(2,1)} %broadcast_in_dim.8), calls=%async_computation | async-start | bytes 262144 | tf_op jit(solution)/shard_map/all_to_all | solution.py:258
  17.9 1.9 %stage.1 = (bf16[2,3072,128]{2,1,0:T(8,128)(2,1)S(1)}, bf16[2,3072,128]{2,1,0:T(8,128)(2,1)S(1)}, bf16[2,16,128]{2,1,0:T(8,128)(2,1)S(1)}, bf16[2,16,128]{2,1,0:T(8,128)(2,1)S(1)}, s32[1,16]{1,0:T(1,128)S(1)}) custom-call(bf16[2,3072,128]{2,1,0:T(8,128)(2,1)} %bitcast.9, bf16[2,3072,128]{2,1,0:T(8,128)(2,1)} %bitcast.10, bf16[2,16,128]{2,1,0:T(8,128)(2,1)} %bitcast.11, ...), custom_call_target="tpu_custom_call" | custom-call | bytes 6324288 | tf_op jit(solution)/shard_map/stage/pallas_call | solution.py:179
  19.9 9.5 %all-to-all-done.q_ref = bf16[32,16,128]{2,1,0:T(8,128)(2,1)S(1)} async-done(((bf16[32,16,128]{2,1,0:T(8,128)(2,1)}), bf16[32,16,128]{2,1,0:T(8,128)(2,1)S(1)}, u32[]{:S(2)}, u32[]{:S(2)}) %all-to-all-start) | async-done | bytes 131104 | tf_op jit(solution)/shard_map/all_to_all | solution.py:258
  29.4 2.7 %attend.1 = bf16[4,144,128]{2,1,0:T(8,128)(2,1)S(1)} custom-call(s32[1]{0:T(128)S(6)} %copy.9.length, bf16[32,16,128]{2,1,0:T(8,128)(2,1)S(1)} %all-to-all-done.q_ref, bf16[2,3072,128]{2,1,0:T(8,128)(2,1)S(1)} %get-tuple-element.10.keys, bf16[2,3072,128]{2,1,0:T(8,128)(2,1)S(1)} %get-tuple-element.11.values, ...), custom_call_target="tpu_custom_call" | custom-call | flops 805306368 | bytes 3145728 | tf_op jit(solution)/shard_map/attend/pallas_call | solution.py:196
  32.1 0.0 copy-start
  32.1 7.5 %all_to_all.20.r_ref = bf16[4,144,128]{2,1,0:T(8,128)(2,1)S(1)} all-to-all(bf16[4,144,128]{2,1,0:T(8,128)(2,1)S(1)} %attend.1), channel_id=1, replica_groups=mesh['x'=4,'za'=4,'zb'=2,'zh'=2,'core'=2,'y'=4] {'x'}, dimensions={0} | all-to-all | bytes 294912 | tf_op jit(solution)/shard_map/all_to_all | solution.py:261
  39.6 0.3 combine.1
  39.9 15.7 %all_to_all.21.r_ref = bf16[8,80,128]{2,1,0:T(8,128)(2,1)S(1)} all-to-all(bf16[8,80,128]{2,1,0:T(8,128)(2,1)S(1)} %combine.1), channel_id=1, replica_groups=mesh['x'=4,'za'=4,'zb'=2,'zh'=2,'core'=2,'y'=4] {'za','zb'}, dimensions={0} | all-to-all | bytes 327680 | tf_op jit(solution)/shard_map/all_to_all | solution.py:263
  55.6 0.3 combine_last.1
  55.9 14.0 %all_to_all.22 = bf16[32,64,128]{2,1,0:T(8,128)(2,1)S(1)} all-to-all(bf16[32,64,128]{2,1,0:T(8,128)(2,1)S(1)} %combine_last.1), channel_id=1, replica_groups=mesh['x'=4,'za'=4,'zb'=2,'zh'=2,'core'=2,'y'=4] {'zb','x','y'}, dimensions={0} | all-to-all | bytes 1048576 | tf_op jit(solution)/shard_map/all_to_all | solution.py:267
  70.0 0.0 copy-done
  70.0 0.3 project.1
  70.3 19.1 %all-gather = bf16[16,16,128]{2,1,0:T(8,128)(2,1)S(1)} all-gather(bf16[4,16,128]{2,1,0:T(8,128)(2,1)S(1)} %project.1), channel_id=2, replica_groups=mesh['x'=4,'za'=4,'zb'=2,'zh'=2,'core'=2,'y'=4] {'zh','core'}, dimensions={0}, use_global_device_ids=true | all-gather | bytes 81920 | tf_op jit(solution)/shard_map/all_gather | solution.py:269
  89.4 0.6 total.1
Async XLA Ops:
  1.3 28.1 %all-to-all-start = ((bf16[32,16,128]{2,1,0:T(8,128)(2,1)}), bf16[32,16,128]{2,1,0:T(8,128)(2,1)S(1)}, u32[]{:S(2)}, u32[]{:S(2)}) async-start(bf16[32,16,128]{2,1,0:T(8,128)(2,1)} %broadcast_in_dim.8), calls=%async_computation | async-start | bytes 262144 | tf_op jit(solution)/shard_map/all_to_all | solution.py:258
  32.1 37.9 %copy-start = (bf16[4096,128]{1,0:T(8,128)(2,1)S(1)}, bf16[4096,128]{1,0:T(8,128)(2,1)}, u32[]{:S(2)}) copy-start(bf16[4096,128]{1,0:T(8,128)(2,1)} %w_ref.1) | copy-start | bytes 3145732

commit v5 on v4

--- a/solution.py
+++ b/solution.py
@@ -62,7 +62,8 @@
     token = dest % NEW
     n_x = lax.axis_size("x")
     n_pairs = NEW // n_x
-    source = (token % n_pairs * n_x + token // n_pairs) * half_rows + dest // NEW
+    place = (token + n_pairs // 2) % n_pairs
+    source = (place * n_x + token // n_pairs) * half_rows + dest // NEW
     order = jnp.where(iota((n, n), 1) == source, 1.0, 0.0).astype(BF)
     arrived = q_ref[...].astype(F32).reshape(n_pairs, 2, n_x, heads * half_rows, size)
 
@@ -78,13 +79,18 @@
     def finish(k, acc, top):
         total = acc[:, size:]
         attended = (acc[:, :size] / total).astype(BF)
+        lane = iota((size, size), 1)
+        half = size // 2
         for h in range(2):
-            part_rows = slice(h * 128, (h + 1) * 128)
-            lane = iota((128, 128), 1)
-            cols = jnp.where(lane == 0, top[part_rows], total[part_rows])
-            stats = jnp.transpose(cols)
-            out_ref[2 * k + h, 0:128, :] = attended[part_rows]
-            out_ref[2 * k + h, 128:, :] = pack_stats(stats[0:1], stats[1:2])
+            part_rows = slice(h * size, (h + 1) * size)
+            stats = jnp.transpose(jnp.where(lane == 0, top[part_rows], total[part_rows]))
+            row_top, row_total = stats[0:1], stats[1:2]
+            for p in range(2):
+                if p:
+                    row_top, row_total = (jnp.concatenate([v[:, half:], v[:, :half]], axis=1) for v in (row_top, row_total))
+                start = h * size + p * half
+                out_ref[4 * k + 2 * h + p, 0:half, :] = attended[start : start + half]
+                out_ref[4 * k + 2 * h + p, half:, :] = pack_stats(row_top, row_total)
 
     tops = []
     for k in range(heads):
@@ -129,18 +135,11 @@
     for s in range(sources):
         out = out + factors[0:rows, s : s + 1] * r_ref[s, 0:rows, :].astype(F32)
     out = out.astype(BF)
-    if last:
-        for c in range(copies):
-            out_ref[c] = out
-        return
-    half = rows // 2
-    for h in range(2):
-        if h:
-            top, total = (jnp.concatenate([v[:, half:], v[:, :half]], axis=1) for v in (top, total))
-        tail = pack_stats(top, total)
-        for c in range(h, copies, 2):
-            out_ref[c, 0:half, :] = out[h * half : (h + 1) * half]
-            out_ref[c, half:, :] = tail
+    tail = None if last else pack_stats(top, total)
+    for c in range(copies):
+        out_ref[c, 0:rows, :] = out
+        if not last:
+            out_ref[c, rows:, :] = tail
 
 
 def project_kernel(r_ref, w_ref, out_ref):
@@ -162,6 +161,10 @@
     out_ref[...] = acc.astype(BF).reshape(out_ref.shape)
 
 
+def from_middle(count):
+    return [[(n + count // 2) % count for n in range(count)]]
+
+
 def in_vmem(n):
     return [pl.BlockSpec(memory_space=pltpu.VMEM)] * n
 
@@ -195,7 +198,7 @@
     flops = 4 * heads * NEW * QPK * slots * size
     return pl.pallas_call(
         functools.partial(attend_kernel, rate=rate, chunk=chunk),
-        out_shape=jax.ShapeDtypeStruct((2 * heads, 128 + STAT_ROWS, size), BF),
+        out_shape=jax.ShapeDtypeStruct((4 * heads, size // 2 + STAT_ROWS, size), BF),
         in_specs=[pl.BlockSpec(memory_space=pltpu.SMEM)] + in_vmem(6),
         out_specs=pl.BlockSpec(memory_space=pltpu.VMEM),
         scratch_shapes=[pltpu.VMEM((heads, NEW * QPK, slots), F32)],
@@ -208,7 +211,7 @@
 
 
 def combine(r, copies, last, rate):
-    rows = r.shape[1] - STAT_ROWS if last else (r.shape[1] - STAT_ROWS) // 2 + STAT_ROWS
+    rows = r.shape[1] - STAT_ROWS if last else r.shape[1]
     return pl.pallas_call(
         functools.partial(combine_kernel, rate=rate, last=last),
         out_shape=jax.ShapeDtypeStruct((copies, rows, r.shape[2]), BF),
@@ -255,12 +258,12 @@
     n_ctx = lax.axis_size(CTX)
     mine = queries[0].reshape(1, -1, size)
     sent = jnp.broadcast_to(mine, (n_ctx,) + mine.shape[1:])
-    q = lax.all_to_all(sent, Z + ("x",), 0, 0, tiled=True)
+    q = lax.all_to_all(sent, Z + ("x",), 0, 0, axis_index_groups=from_middle(n_ctx), tiled=True)
     staged = stage(cache_keys[0], cache_values[0], new_keys[0], new_values[0], positions)
     part = attend(lengths, q, *staged)
-    part = lax.all_to_all(part, "x", 0, 0, tiled=True)
-    part = combine(part, lax.axis_size(Z), False, rate)
-    part = lax.all_to_all(part, Z, 0, 0, tiled=True)
+    part = lax.all_to_all(part, ("x", "zb"), 0, 0, tiled=True)
+    part = combine(part, lax.axis_size("za"), False, rate)
+    part = lax.all_to_all(part, "za", 0, 0, axis_index_groups=from_middle(lax.axis_size("za")), tiled=True)
     spread = ("zb", "x", "y")
     sizes = tuple(lax.axis_size(a) for a in spread)
     rows = combine(part, math.prod(sizes), True, rate)

time: 90.3 us -> 82.7 us (0.916)
  waiting for transfers between devices: 9.54 us -> 4.6 us
  blocking collectives: 56.3 us -> 53.5 us
    all_to_all x2, blocking collectives: 23.2 us -> 18.2 us  [the longest x1 9.9 us: body(): lax.all_to_all(part, 'za', 0, 0, axis_index_groups=from_middle(lax.axis_s...]
    all_to_all x1, waiting for transfers between devices: 9.54 us -> 4.6 us  [body(): lax.all_to_all(sent, Z + ('x',), 0, 0, axis_index_groups=from_middle(n_ct...]
    all_gather x1, blocking collectives: 19.1 us -> 20.9 us  [body(): every = lax.all_gather(out, HEAD, axis=0)]
where the time goes in v5:
time: 82.7 us; the launch traced here: 82.3 us
  blocking collectives  53.5 us (65%)
  starting transfers between devices  16 us (19%)
  Pallas kernels  6.23 us (8%)
  waiting for transfers between devices  4.6 us (6%)
  local copies, waits for them, and re-layouts  1.35 us (2%)
    all_gather x1, blocking collectives, body(): every = lax.all_gather(out, HEAD, axis=0)  20.9 us
    all_to_all x1, starting transfers between devices, body(): lax.all_to_all(sent, Z + ('x',), 0, 0, axis_index_groups=from_middle(n_ct...  16 us
    all_to_all x1, blocking collectives, body(): rows = lax.all_to_all(rows, spread, 0, 0, tiled=True)  14.4 us
    all_to_all x1, blocking collectives, body(): lax.all_to_all(part, 'za', 0, 0, axis_index_groups=from_middle(lax.axis_s...  9.9 us
    all_to_all x1, blocking collectives, body(): part = lax.all_to_all(part, ('x', 'zb'), 0, 0, tiled=True)  8.28 us
    all_to_all x1, waiting for transfers between devices, body(): lax.all_to_all(sent, Z + ('x',), 0, 0, axis_index_groups=from_middle(n_ct...  4.6 us
    pallas_call x1, Pallas kernels, attend(): pl.pallas_call(functools.partial(attend_kernel, rate=rate, chunk=chunk),...  2.83 us
    pallas_call x1, Pallas kernels, stage(): pl.pallas_call(stage_kernel, out_shape=[jax.ShapeDtypeStruct(a.shape, a.d...  1.94 us
  transfers between devices with their start and end apart: 1, of which 1 were waited for; matrix products, arithmetic and copies ran while one was open for 0% of the time, Pallas kernels for 2%

profile of v5, /device:TPU:1, one launch (start us, length us, event | category | flops | bytes accessed | tf_op | source)
XLA Modules:
  0.0 82.3 jit_solution(6497162278381287183)
XLA Ops:
  0.0 1.3 %broadcast_in_dim.8 = bf16[32,16,128]{2,1,0:T(8,128)(2,1)} broadcast(bf16[16,128]{1,0:T(8,128)(2,1)} %bitcast.13), dimensions={1,2} | broadcast | bytes 135168 | tf_op jit(solution)/shard_map/broadcast_in_dim | solution.py:260
  1.3 16.0 %all-to-all-start = ((bf16[32,16,128]{2,1,0:T(8,128)(2,1)}), bf16[32,16,128]{2,1,0:T(8,128)(2,1)S(1)}, u32[]{:S(2)}, u32[]{:S(2)}) async-start(bf16[32,16,128]{2,1,0:T(8,128)(2,1)} %broadcast_in_dim.8), calls=%async_computation | async-start | bytes 262144 | tf_op jit(solution)/shard_map/all_to_all | solution.py:261
  18.0 1.9 %stage.1 = (bf16[2,3072,128]{2,1,0:T(8,128)(2,1)S(1)}, bf16[2,3072,128]{2,1,0:T(8,128)(2,1)S(1)}, bf16[2,16,128]{2,1,0:T(8,128)(2,1)S(1)}, bf16[2,16,128]{2,1,0:T(8,128)(2,1)S(1)}, s32[1,16]{1,0:T(1,128)S(1)}) custom-call(bf16[2,3072,128]{2,1,0:T(8,128)(2,1)} %bitcast.9, bf16[2,3072,128]{2,1,0:T(8,128)(2,1)} %bitcast.10, bf16[2,16,128]{2,1,0:T(8,128)(2,1)} %bitcast.11, ...), custom_call_target="tpu_custom_call" | custom-call | bytes 6324288 | tf_op jit(solution)/shard_map/stage/pallas_call | solution.py:182
  19.9 4.6 %all-to-all-done.q_ref = bf16[32,16,128]{2,1,0:T(8,128)(2,1)S(1)} async-done(((bf16[32,16,128]{2,1,0:T(8,128)(2,1)}), bf16[32,16,128]{2,1,0:T(8,128)(2,1)S(1)}, u32[]{:S(2)}, u32[]{:S(2)}) %all-to-all-start) | async-done | bytes 131104 | tf_op jit(solution)/shard_map/all_to_all | solution.py:261
  24.5 2.8 %attend.1 = bf16[8,80,128]{2,1,0:T(8,128)(2,1)S(1)} custom-call(s32[1]{0:T(128)S(6)} %copy.9.length, bf16[32,16,128]{2,1,0:T(8,128)(2,1)S(1)} %all-to-all-done.q_ref, bf16[2,3072,128]{2,1,0:T(8,128)(2,1)S(1)} %get-tuple-element.10.keys, bf16[2,3072,128]{2,1,0:T(8,128)(2,1)S(1)} %get-tuple-element.11.values, ...), custom_call_target="tpu_custom_call" | custom-call | flops 805306368 | bytes 3145728 | tf_op jit(solution)/shard_map/attend/pallas_call | solution.py:199
  27.4 0.0 copy-start
  27.4 8.3 %all_to_all.20.r_ref = bf16[8,80,128]{2,1,0:T(8,128)(2,1)S(1)} all-to-all(bf16[8,80,128]{2,1,0:T(8,128)(2,1)S(1)} %attend.1), channel_id=1, replica_groups=mesh['x'=4,'za'=4,'zb'=2,'zh'=2,'core'=2,'y'=4] {'x','zb'}, dimensions={0} | all-to-all | bytes 327680 | tf_op jit(solution)/shard_map/all_to_all | solution.py:264
  35.6 0.3 combine.1
  35.9 9.9 %all_to_all.21.r_ref = bf16[4,80,128]{2,1,0:T(8,128)(2,1)S(1)} all-to-all(bf16[4,80,128]{2,1,0:T(8,128)(2,1)S(1)} %combine.1), channel_id=1, replica_groups={{64,96,0,32},{65,97,1,33},{66,98,2,34},{67,99,3,35},{68,100,4,36},{69,1..., dimensions={0} | all-to-all | bytes 163840 | tf_op jit(solution)/shard_map/all_to_all | solution.py:266
  45.8 0.3 combine_last.1
  46.1 14.4 %all_to_all.22 = bf16[32,64,128]{2,1,0:T(8,128)(2,1)S(1)} all-to-all(bf16[32,64,128]{2,1,0:T(8,128)(2,1)S(1)} %combine_last.1), channel_id=1, replica_groups=mesh['x'=4,'za'=4,'zb'=2,'zh'=2,'core'=2,'y'=4] {'zb','x','y'}, dimensions={0} | all-to-all | bytes 1048576 | tf_op jit(solution)/shard_map/all_to_all | solution.py:270
  60.5 0.0 copy-done
  60.5 0.3 project.1
  60.8 20.9 %all-gather = bf16[16,16,128]{2,1,0:T(8,128)(2,1)S(1)} all-gather(bf16[4,16,128]{2,1,0:T(8,128)(2,1)S(1)} %project.1), channel_id=2, replica_groups=mesh['x'=4,'za'=4,'zb'=2,'zh'=2,'core'=2,'y'=4] {'zh','core'}, dimensions={0}, use_global_device_ids=true | all-gather | bytes 81920 | tf_op jit(solution)/shard_map/all_gather | solution.py:272
  81.7 0.6 total.1
Async XLA Ops:
  1.3 23.2 %all-to-all-start = ((bf16[32,16,128]{2,1,0:T(8,128)(2,1)}), bf16[32,16,128]{2,1,0:T(8,128)(2,1)S(1)}, u32[]{:S(2)}, u32[]{:S(2)}) async-start(bf16[32,16,128]{2,1,0:T(8,128)(2,1)} %broadcast_in_dim.8), calls=%async_computation | async-start | bytes 262144 | tf_op jit(solution)/shard_map/all_to_all | solution.py:261
  27.4 33.1 %copy-start = (bf16[4096,128]{1,0:T(8,128)(2,1)S(1)}, bf16[4096,128]{1,0:T(8,128)(2,1)}, u32[]{:S(2)}) copy-start(bf16[4096,128]{1,0:T(8,128)(2,1)} %w_ref.1) | copy-start | bytes 3145732

commit v6 on v5

--- a/solution.py
+++ b/solution.py
@@ -63,12 +63,12 @@
     n_x = lax.axis_size("x")
     n_pairs = NEW // n_x
     place = (token + n_pairs // 2) % n_pairs
-    source = (place * n_x + token // n_pairs) * half_rows + dest // NEW
+    source = (place * n_x + n_x - 1 - token // n_pairs) * half_rows + dest // NEW
     order = jnp.where(iota((n, n), 1) == source, 1.0, 0.0).astype(BF)
     arrived = q_ref[...].astype(F32).reshape(n_pairs, 2, n_x, heads * half_rows, size)
 
     def ordered(k, h):
-        block = arrived[:, h, :, k * half_rows : (k + 1) * half_rows, :].reshape(n, size).astype(BF)
+        block = arrived[:, 1 - h, :, k * half_rows : (k + 1) * half_rows, :].reshape(n, size).astype(BF)
         return jnp.dot(order, block, preferred_element_type=F32).astype(BF)
 
 
@@ -85,12 +85,13 @@
             part_rows = slice(h * size, (h + 1) * size)
             stats = jnp.transpose(jnp.where(lane == 0, top[part_rows], total[part_rows]))
             row_top, row_total = stats[0:1], stats[1:2]
+            first = out_ref.shape[0] - 2 * (2 * k + h + 1)
             for p in range(2):
                 if p:
                     row_top, row_total = (jnp.concatenate([v[:, half:], v[:, :half]], axis=1) for v in (row_top, row_total))
                 start = h * size + p * half
-                out_ref[4 * k + 2 * h + p, 0:half, :] = attended[start : start + half]
-                out_ref[4 * k + 2 * h + p, half:, :] = pack_stats(row_top, row_total)
+                out_ref[first + p, 0:half, :] = attended[start : start + half]
+                out_ref[first + p, half:, :] = pack_stats(row_top, row_total)
 
     tops = []
     for k in range(heads):
@@ -151,7 +152,7 @@
             for j in range(0, per, 2):
                 block = jnp.concatenate(
                     [
-                        jnp.concatenate([r_ref[z, x, y, pl.ds((j + i) * NEW, NEW), :] for y in range(n_y)], axis=0)
+                        jnp.concatenate([r_ref[z, n_x - 1 - x, n_y - 1 - y, pl.ds((j + i) * NEW, NEW), :] for y in range(n_y)], axis=0)
                         for i in range(2)
                     ],
                     axis=1,
@@ -161,8 +162,8 @@
     out_ref[...] = acc.astype(BF).reshape(out_ref.shape)
 
 
-def from_middle(count):
-    return [[(n + count // 2) % count for n in range(count)]]
+def listed(count, flip):
+    return [[n ^ flip for n in range(count)]]
 
 
 def in_vmem(n):
@@ -258,18 +259,18 @@
     n_ctx = lax.axis_size(CTX)
     mine = queries[0].reshape(1, -1, size)
     sent = jnp.broadcast_to(mine, (n_ctx,) + mine.shape[1:])
-    q = lax.all_to_all(sent, Z + ("x",), 0, 0, axis_index_groups=from_middle(n_ctx), tiled=True)
+    q = lax.all_to_all(sent, Z + ("x",), 0, 0, axis_index_groups=listed(n_ctx, 23), tiled=True)
     staged = stage(cache_keys[0], cache_values[0], new_keys[0], new_values[0], positions)
     part = attend(lengths, q, *staged)
-    part = lax.all_to_all(part, ("x", "zb"), 0, 0, tiled=True)
+    part = lax.all_to_all(part, ("x", "zb"), 0, 0, axis_index_groups=listed(part.shape[0], 6), tiled=True)
     part = combine(part, lax.axis_size("za"), False, rate)
-    part = lax.all_to_all(part, "za", 0, 0, axis_index_groups=from_middle(lax.axis_size("za")), tiled=True)
+    part = lax.all_to_all(part, "za", 0, 0, axis_index_groups=listed(part.shape[0], 2), tiled=True)
     spread = ("zb", "x", "y")
     sizes = tuple(lax.axis_size(a) for a in spread)
     rows = combine(part, math.prod(sizes), True, rate)
-    rows = lax.all_to_all(rows, spread, 0, 0, tiled=True)
+    rows = lax.all_to_all(rows, spread, 0, 0, axis_index_groups=listed(rows.shape[0], 15), tiled=True)
     out = project(rows.reshape(*sizes, *rows.shape[1:]), out_weight)
-    every = lax.all_gather(out, HEAD, axis=0)
+    every = lax.all_gather(out, HEAD, axis=0, axis_index_groups=listed(lax.axis_size(HEAD), 2))
     return total_of(every)
 
 

time: 82.7 us -> 81.4 us (0.984)
  waiting for transfers between devices: 4.6 us -> 3.25 us
    all_to_all x1, waiting for transfers between devices: 4.6 us -> 3.25 us  [body(): lax.all_to_all(sent, Z + ('x',), 0, 0, axis_index_groups=listed(n_ctx, 23...]
where the time goes in v6:
time: 81.4 us; the launch traced here: 81.1 us
  blocking collectives  53 us (65%)
  starting transfers between devices  16.6 us (20%)
  Pallas kernels  6.23 us (8%)
  waiting for transfers between devices  3.25 us (4%)
  local copies, waits for them, and re-layouts  1.35 us (2%)
    all_gather x1, blocking collectives, body(): lax.all_gather(out, HEAD, axis=0, axis_index_groups=listed(lax.axis_size(...  20.8 us
    all_to_all x1, starting transfers between devices, body(): lax.all_to_all(sent, Z + ('x',), 0, 0, axis_index_groups=listed(n_ctx, 23...  16.6 us
    all_to_all x1, blocking collectives, body(): lax.all_to_all(rows, spread, 0, 0, axis_index_groups=listed(rows.shape[0]...  14.2 us
    all_to_all x1, blocking collectives, body(): lax.all_to_all(part, 'za', 0, 0, axis_index_groups=listed(part.shape[0],...  9.9 us
    all_to_all x1, blocking collectives, body(): lax.all_to_all(part, ('x', 'zb'), 0, 0, axis_index_groups=listed(part.sha...  8.12 us
    all_to_all x1, waiting for transfers between devices, body(): lax.all_to_all(sent, Z + ('x',), 0, 0, axis_index_groups=listed(n_ctx, 23...  3.25 us
    pallas_call x1, Pallas kernels, attend(): pl.pallas_call(functools.partial(attend_kernel, rate=rate, chunk=chunk),...  2.82 us
    pallas_call x1, Pallas kernels, stage(): pl.pallas_call(stage_kernel, out_shape=[jax.ShapeDtypeStruct(a.shape, a.d...  1.94 us
  transfers between devices with their start and end apart: 1, of which 1 were waited for; matrix products, arithmetic and copies ran while one was open for 0% of the time, Pallas kernels for 2%

profile of v6, /device:TPU:1, one launch (start us, length us, event | category | flops | bytes accessed | tf_op | source)
XLA Modules:
  0.0 81.1 jit_solution(421354048874876884)
XLA Ops:
  0.0 1.3 %broadcast_in_dim.8 = bf16[32,16,128]{2,1,0:T(8,128)(2,1)} broadcast(bf16[16,128]{1,0:T(8,128)(2,1)} %bitcast.13), dimensions={1,2} | broadcast | bytes 135168 | tf_op jit(solution)/shard_map/broadcast_in_dim | solution.py:261
  1.3 16.6 %all-to-all-start = ((bf16[32,16,128]{2,1,0:T(8,128)(2,1)}), bf16[32,16,128]{2,1,0:T(8,128)(2,1)S(1)}, u32[]{:S(2)}, u32[]{:S(2)}) async-start(bf16[32,16,128]{2,1,0:T(8,128)(2,1)} %broadcast_in_dim.8), calls=%async_computation | async-start | bytes 262144 | tf_op jit(solution)/shard_map/all_to_all | solution.py:262
  18.6 1.9 %stage.1 = (bf16[2,3072,128]{2,1,0:T(8,128)(2,1)S(1)}, bf16[2,3072,128]{2,1,0:T(8,128)(2,1)S(1)}, bf16[2,16,128]{2,1,0:T(8,128)(2,1)S(1)}, bf16[2,16,128]{2,1,0:T(8,128)(2,1)S(1)}, s32[1,16]{1,0:T(1,128)S(1)}) custom-call(bf16[2,3072,128]{2,1,0:T(8,128)(2,1)} %bitcast.9, bf16[2,3072,128]{2,1,0:T(8,128)(2,1)} %bitcast.10, bf16[2,16,128]{2,1,0:T(8,128)(2,1)} %bitcast.11, ...), custom_call_target="tpu_custom_call" | custom-call | bytes 6324288 | tf_op jit(solution)/shard_map/stage/pallas_call | solution.py:183
  20.5 3.3 %all-to-all-done.q_ref = bf16[32,16,128]{2,1,0:T(8,128)(2,1)S(1)} async-done(((bf16[32,16,128]{2,1,0:T(8,128)(2,1)}), bf16[32,16,128]{2,1,0:T(8,128)(2,1)S(1)}, u32[]{:S(2)}, u32[]{:S(2)}) %all-to-all-start) | async-done | bytes 131104 | tf_op jit(solution)/shard_map/all_to_all | solution.py:262
  23.8 2.8 %attend.1 = bf16[8,80,128]{2,1,0:T(8,128)(2,1)S(1)} custom-call(s32[1]{0:T(128)S(6)} %copy.9.length, bf16[32,16,128]{2,1,0:T(8,128)(2,1)S(1)} %all-to-all-done.q_ref, bf16[2,3072,128]{2,1,0:T(8,128)(2,1)S(1)} %get-tuple-element.10.keys, bf16[2,3072,128]{2,1,0:T(8,128)(2,1)S(1)} %get-tuple-element.11.values, ...), custom_call_target="tpu_custom_call" | custom-call | flops 805306368 | bytes 3145728 | tf_op jit(solution)/shard_map/attend/pallas_call | solution.py:200
  26.6 0.0 copy-start
  26.6 8.1 %all_to_all.20.r_ref = bf16[8,80,128]{2,1,0:T(8,128)(2,1)S(1)} all-to-all(bf16[8,80,128]{2,1,0:T(8,128)(2,1)S(1)} %attend.1), channel_id=1, replica_groups={{384,400,256,272,128,144,0,16},{385,401,257,273,129,145,1,17},{386,402,..., dimensions={0} | all-to-all | bytes 327680 | tf_op jit(solution)/shard_map/all_to_all | solution.py:265
  34.7 0.3 combine.1
  35.0 9.9 %all_to_all.21.r_ref = bf16[4,80,128]{2,1,0:T(8,128)(2,1)S(1)} all-to-all(bf16[4,80,128]{2,1,0:T(8,128)(2,1)S(1)} %combine.1), channel_id=1, replica_groups={{64,96,0,32},{65,97,1,33},{66,98,2,34},{67,99,3,35},{68,100,4,36},{69,1..., dimensions={0} | all-to-all | bytes 163840 | tf_op jit(solution)/shard_map/all_to_all | solution.py:267
  44.9 0.3 combine_last.1
  45.2 14.2 %all_to_all.22 = bf16[32,64,128]{2,1,0:T(8,128)(2,1)S(1)} all-to-all(bf16[32,64,128]{2,1,0:T(8,128)(2,1)S(1)} %combine_last.1), channel_id=1, replica_groups={{387,386,385,384,259,258,257,256,131,130,129,128,3,2,1,0,403,402,401,40..., dimensions={0} | all-to-all | bytes 1048576 | tf_op jit(solution)/shard_map/all_to_all | solution.py:271
  59.4 0.0 copy-done
  59.4 0.3 project.1
  59.7 20.8 %all-gather = bf16[16,16,128]{2,1,0:T(8,128)(2,1)S(1)} all-gather(bf16[4,16,128]{2,1,0:T(8,128)(2,1)S(1)} %project.1), channel_id=2, replica_groups={{8,12,0,4},{9,13,1,5},{10,14,2,6},{11,15,3,7},{24,28,16,20},{25,29,17,2..., dimensions={0}, use_global_device_ids=true | all-gather | bytes 81920 | tf_op jit(solution)/shard_map/all_gather | solution.py:273
  80.5 0.6 total.1
Async XLA Ops:
  1.3 22.4 %all-to-all-start = ((bf16[32,16,128]{2,1,0:T(8,128)(2,1)}), bf16[32,16,128]{2,1,0:T(8,128)(2,1)S(1)}, u32[]{:S(2)}, u32[]{:S(2)}) async-start(bf16[32,16,128]{2,1,0:T(8,128)(2,1)} %broadcast_in_dim.8), calls=%async_computation | async-start | bytes 262144 | tf_op jit(solution)/shard_map/all_to_all | solution.py:262
  26.6 32.8 %copy-start = (bf16[4096,128]{1,0:T(8,128)(2,1)S(1)}, bf16[4096,128]{1,0:T(8,128)(2,1)}, u32[]{:S(2)}) copy-start(bf16[4096,128]{1,0:T(8,128)(2,1)} %w_ref.1) | copy-start | bytes 3145732

commit v7 on v6

--- a/solution.py
+++ b/solution.py
@@ -85,13 +85,14 @@
             part_rows = slice(h * size, (h + 1) * size)
             stats = jnp.transpose(jnp.where(lane == 0, top[part_rows], total[part_rows]))
             row_top, row_total = stats[0:1], stats[1:2]
-            first = out_ref.shape[0] - 2 * (2 * k + h + 1)
+            quarters = out_ref.shape[0] // 2
+            first = quarters - 1 - (2 * k + h)
             for p in range(2):
                 if p:
                     row_top, row_total = (jnp.concatenate([v[:, half:], v[:, :half]], axis=1) for v in (row_top, row_total))
                 start = h * size + p * half
-                out_ref[first + p, 0:half, :] = attended[start : start + half]
-                out_ref[first + p, half:, :] = pack_stats(row_top, row_total)
+                out_ref[p * quarters + first, 0:half, :] = attended[start : start + half]
+                out_ref[p * quarters + first, half:, :] = pack_stats(row_top, row_total)
 
     tops = []
     for k in range(heads):
@@ -152,7 +153,7 @@
             for j in range(0, per, 2):
                 block = jnp.concatenate(
                     [
-                        jnp.concatenate([r_ref[z, n_x - 1 - x, n_y - 1 - y, pl.ds((j + i) * NEW, NEW), :] for y in range(n_y)], axis=0)
+                        jnp.concatenate([r_ref[z, (x + n_x // 2) % n_x, (y + n_y // 2) % n_y, pl.ds((j + i) * NEW, NEW), :] for y in range(n_y)], axis=0)
                         for i in range(2)
                     ],
                     axis=1,
@@ -262,13 +263,13 @@
     q = lax.all_to_all(sent, Z + ("x",), 0, 0, axis_index_groups=listed(n_ctx, 23), tiled=True)
     staged = stage(cache_keys[0], cache_values[0], new_keys[0], new_values[0], positions)
     part = attend(lengths, q, *staged)
-    part = lax.all_to_all(part, ("x", "zb"), 0, 0, axis_index_groups=listed(part.shape[0], 6), tiled=True)
+    part = lax.all_to_all(part, ("zb", "x"), 0, 0, axis_index_groups=listed(part.shape[0], 3), tiled=True)
     part = combine(part, lax.axis_size("za"), False, rate)
     part = lax.all_to_all(part, "za", 0, 0, axis_index_groups=listed(part.shape[0], 2), tiled=True)
     spread = ("zb", "x", "y")
     sizes = tuple(lax.axis_size(a) for a in spread)
     rows = combine(part, math.prod(sizes), True, rate)
-    rows = lax.all_to_all(rows, spread, 0, 0, axis_index_groups=listed(rows.shape[0], 15), tiled=True)
+    rows = lax.all_to_all(rows, spread, 0, 0, axis_index_groups=listed(rows.shape[0], 10), tiled=True)
     out = project(rows.reshape(*sizes, *rows.shape[1:]), out_weight)
     every = lax.all_gather(out, HEAD, axis=0, axis_index_groups=listed(lax.axis_size(HEAD), 2))
     return total_of(every)

time: 81.4 us -> 80.3 us (0.986)
  blocking collectives: 53 us -> 51.9 us
where the time goes in v7:
time: 80.3 us; the launch traced here: 80 us
  blocking collectives  51.9 us (65%)
  starting transfers between devices  16.6 us (21%)
  Pallas kernels  6.23 us (8%)
  waiting for transfers between devices  3.25 us (4%)
  local copies, waits for them, and re-layouts  1.35 us (2%)
    all_gather x1, blocking collectives, body(): lax.all_gather(out, HEAD, axis=0, axis_index_groups=listed(lax.axis_size(...  20.5 us
    all_to_all x1, starting transfers between devices, body(): lax.all_to_all(sent, Z + ('x',), 0, 0, axis_index_groups=listed(n_ctx, 23...  16.6 us
    all_to_all x1, blocking collectives, body(): lax.all_to_all(rows, spread, 0, 0, axis_index_groups=listed(rows.shape[0]...  13.4 us
    all_to_all x1, blocking collectives, body(): lax.all_to_all(part, 'za', 0, 0, axis_index_groups=listed(part.shape[0],...  9.9 us
    all_to_all x1, blocking collectives, body(): lax.all_to_all(part, ('zb', 'x'), 0, 0, axis_index_groups=listed(part.sha...  8.12 us
    all_to_all x1, waiting for transfers between devices, body(): lax.all_to_all(sent, Z + ('x',), 0, 0, axis_index_groups=listed(n_ctx, 23...  3.25 us
    pallas_call x1, Pallas kernels, attend(): pl.pallas_call(functools.partial(attend_kernel, rate=rate, chunk=chunk),...  2.82 us
    pallas_call x1, Pallas kernels, stage(): pl.pallas_call(stage_kernel, out_shape=[jax.ShapeDtypeStruct(a.shape, a.d...  1.94 us
  transfers between devices with their start and end apart: 1, of which 1 were waited for; matrix products, arithmetic and copies ran while one was open for 0% of the time, Pallas kernels for 2%

profile of v7, /device:TPU:1, one launch (start us, length us, event | category | flops | bytes accessed | tf_op | source)
XLA Modules:
  0.0 80.0 jit_solution(6500733756169962146)
XLA Ops:
  0.0 1.3 %broadcast_in_dim.8 = bf16[32,16,128]{2,1,0:T(8,128)(2,1)} broadcast(bf16[16,128]{1,0:T(8,128)(2,1)} %bitcast.13), dimensions={1,2} | broadcast | bytes 135168 | tf_op jit(solution)/shard_map/broadcast_in_dim | solution.py:262
  1.3 16.6 %all-to-all-start = ((bf16[32,16,128]{2,1,0:T(8,128)(2,1)}), bf16[32,16,128]{2,1,0:T(8,128)(2,1)S(1)}, u32[]{:S(2)}, u32[]{:S(2)}) async-start(bf16[32,16,128]{2,1,0:T(8,128)(2,1)} %broadcast_in_dim.8), calls=%async_computation | async-start | bytes 262144 | tf_op jit(solution)/shard_map/all_to_all | solution.py:263
  18.6 1.9 %stage.1 = (bf16[2,3072,128]{2,1,0:T(8,128)(2,1)S(1)}, bf16[2,3072,128]{2,1,0:T(8,128)(2,1)S(1)}, bf16[2,16,128]{2,1,0:T(8,128)(2,1)S(1)}, bf16[2,16,128]{2,1,0:T(8,128)(2,1)S(1)}, s32[1,16]{1,0:T(1,128)S(1)}) custom-call(bf16[2,3072,128]{2,1,0:T(8,128)(2,1)} %bitcast.9, bf16[2,3072,128]{2,1,0:T(8,128)(2,1)} %bitcast.10, bf16[2,16,128]{2,1,0:T(8,128)(2,1)} %bitcast.11, ...), custom_call_target="tpu_custom_call" | custom-call | bytes 6324288 | tf_op jit(solution)/shard_map/stage/pallas_call | solution.py:184
  20.5 3.3 %all-to-all-done.q_ref = bf16[32,16,128]{2,1,0:T(8,128)(2,1)S(1)} async-done(((bf16[32,16,128]{2,1,0:T(8,128)(2,1)}), bf16[32,16,128]{2,1,0:T(8,128)(2,1)S(1)}, u32[]{:S(2)}, u32[]{:S(2)}) %all-to-all-start) | async-done | bytes 131104 | tf_op jit(solution)/shard_map/all_to_all | solution.py:263
  23.8 2.8 %attend.1 = bf16[8,80,128]{2,1,0:T(8,128)(2,1)S(1)} custom-call(s32[1]{0:T(128)S(6)} %copy.9.length, bf16[32,16,128]{2,1,0:T(8,128)(2,1)S(1)} %all-to-all-done.q_ref, bf16[2,3072,128]{2,1,0:T(8,128)(2,1)S(1)} %get-tuple-element.10.keys, bf16[2,3072,128]{2,1,0:T(8,128)(2,1)S(1)} %get-tuple-element.11.values, ...), custom_call_target="tpu_custom_call" | custom-call | flops 805306368 | bytes 3145728 | tf_op jit(solution)/shard_map/attend/pallas_call | solution.py:201
  26.6 0.0 copy-start
  26.6 8.1 %all_to_all.20.r_ref = bf16[8,80,128]{2,1,0:T(8,128)(2,1)S(1)} all-to-all(bf16[8,80,128]{2,1,0:T(8,128)(2,1)S(1)} %attend.1), channel_id=1, replica_groups={{384,256,128,0,400,272,144,16},{385,257,129,1,401,273,145,17},{386,258,..., dimensions={0} | all-to-all | bytes 327680 | tf_op jit(solution)/shard_map/all_to_all | solution.py:266
  34.7 0.3 combine.1
  35.0 9.9 %all_to_all.21.r_ref = bf16[4,80,128]{2,1,0:T(8,128)(2,1)S(1)} all-to-all(bf16[4,80,128]{2,1,0:T(8,128)(2,1)S(1)} %combine.1), channel_id=1, replica_groups={{64,96,0,32},{65,97,1,33},{66,98,2,34},{67,99,3,35},{68,100,4,36},{69,1..., dimensions={0} | all-to-all | bytes 163840 | tf_op jit(solution)/shard_map/all_to_all | solution.py:268
  44.9 0.3 combine_last.1
  45.2 13.4 %all_to_all.22 = bf16[32,64,128]{2,1,0:T(8,128)(2,1)S(1)} all-to-all(bf16[32,64,128]{2,1,0:T(8,128)(2,1)S(1)} %combine_last.1), channel_id=1, replica_groups={{258,259,256,257,386,387,384,385,2,3,0,1,130,131,128,129,274,275,272,27..., dimensions={0} | all-to-all | bytes 1048576 | tf_op jit(solution)/shard_map/all_to_all | solution.py:272
  58.6 0.0 copy-done
  58.6 0.3 project.1
  59.0 20.5 %all-gather = bf16[16,16,128]{2,1,0:T(8,128)(2,1)S(1)} all-gather(bf16[4,16,128]{2,1,0:T(8,128)(2,1)S(1)} %project.1), channel_id=2, replica_groups={{8,12,0,4},{9,13,1,5},{10,14,2,6},{11,15,3,7},{24,28,16,20},{25,29,17,2..., dimensions={0}, use_global_device_ids=true | all-gather | bytes 81920 | tf_op jit(solution)/shard_map/all_gather | solution.py:274
  79.4 0.6 total.1
Async XLA Ops:
  1.3 22.4 %all-to-all-start = ((bf16[32,16,128]{2,1,0:T(8,128)(2,1)}), bf16[32,16,128]{2,1,0:T(8,128)(2,1)S(1)}, u32[]{:S(2)}, u32[]{:S(2)}) async-start(bf16[32,16,128]{2,1,0:T(8,128)(2,1)} %broadcast_in_dim.8), calls=%async_computation | async-start | bytes 262144 | tf_op jit(solution)/shard_map/all_to_all | solution.py:263
  26.6 32.0 %copy-start = (bf16[4096,128]{1,0:T(8,128)(2,1)S(1)}, bf16[4096,128]{1,0:T(8,128)(2,1)}, u32[]{:S(2)}) copy-start(bf16[4096,128]{1,0:T(8,128)(2,1)} %w_ref.1) | copy-start | bytes 3145732

commit v8 on v7

--- a/solution.py
+++ b/solution.py
@@ -63,7 +63,7 @@
     n_x = lax.axis_size("x")
     n_pairs = NEW // n_x
     place = (token + n_pairs // 2) % n_pairs
-    source = (place * n_x + n_x - 1 - token // n_pairs) * half_rows + dest // NEW
+    source = (place * n_x + (token // n_pairs + n_x // 2) % n_x) * half_rows + dest // NEW
     order = jnp.where(iota((n, n), 1) == source, 1.0, 0.0).astype(BF)
     arrived = q_ref[...].astype(F32).reshape(n_pairs, 2, n_x, heads * half_rows, size)
 
@@ -86,7 +86,7 @@
             stats = jnp.transpose(jnp.where(lane == 0, top[part_rows], total[part_rows]))
             row_top, row_total = stats[0:1], stats[1:2]
             quarters = out_ref.shape[0] // 2
-            first = quarters - 1 - (2 * k + h)
+            first = (2 * k + h + quarters // 2) % quarters
             for p in range(2):
                 if p:
                     row_top, row_total = (jnp.concatenate([v[:, half:], v[:, :half]], axis=1) for v in (row_top, row_total))
@@ -260,10 +260,10 @@
     n_ctx = lax.axis_size(CTX)
     mine = queries[0].reshape(1, -1, size)
     sent = jnp.broadcast_to(mine, (n_ctx,) + mine.shape[1:])
-    q = lax.all_to_all(sent, Z + ("x",), 0, 0, axis_index_groups=listed(n_ctx, 23), tiled=True)
+    q = lax.all_to_all(sent, Z + ("x",), 0, 0, axis_index_groups=listed(n_ctx, 22), tiled=True)
     staged = stage(cache_keys[0], cache_values[0], new_keys[0], new_values[0], positions)
     part = attend(lengths, q, *staged)
-    part = lax.all_to_all(part, ("zb", "x"), 0, 0, axis_index_groups=listed(part.shape[0], 3), tiled=True)
+    part = lax.all_to_all(part, ("zb", "x"), 0, 0, axis_index_groups=listed(part.shape[0], 2), tiled=True)
     part = combine(part, lax.axis_size("za"), False, rate)
     part = lax.all_to_all(part, "za", 0, 0, axis_index_groups=listed(part.shape[0], 2), tiled=True)
     spread = ("zb", "x", "y")

time: 80.3 us -> 79.7 us (level)
  blocking collectives: 51.9 us -> 50.9 us
where the time goes in v8:
time: 79.7 us; the launch traced here: 79.3 us
  blocking collectives  50.9 us (64%)
  starting transfers between devices  16.6 us (21%)
  Pallas kernels  6.25 us (8%)
  waiting for transfers between devices  3.52 us (4%)
  local copies, waits for them, and re-layouts  1.35 us (2%)
    all_gather x1, blocking collectives, body(): lax.all_gather(out, HEAD, axis=0, axis_index_groups=listed(lax.axis_size(...  19.8 us
    all_to_all x1, starting transfers between devices, body(): lax.all_to_all(sent, Z + ('x',), 0, 0, axis_index_groups=listed(n_ctx, 22...  16.6 us
    all_to_all x1, blocking collectives, body(): lax.all_to_all(rows, spread, 0, 0, axis_index_groups=listed(rows.shape[0]...  13.1 us
    all_to_all x1, blocking collectives, body(): lax.all_to_all(part, 'za', 0, 0, axis_index_groups=listed(part.shape[0],...  10.3 us
    all_to_all x1, blocking collectives, body(): lax.all_to_all(part, ('zb', 'x'), 0, 0, axis_index_groups=listed(part.sha...  7.68 us
    all_to_all x1, waiting for transfers between devices, body(): lax.all_to_all(sent, Z + ('x',), 0, 0, axis_index_groups=listed(n_ctx, 22...  3.52 us
    pallas_call x1, Pallas kernels, attend(): pl.pallas_call(functools.partial(attend_kernel, rate=rate, chunk=chunk),...  2.85 us
    pallas_call x1, Pallas kernels, stage(): pl.pallas_call(stage_kernel, out_shape=[jax.ShapeDtypeStruct(a.shape, a.d...  1.94 us
  transfers between devices with their start and end apart: 1, of which 1 were waited for; matrix products, arithmetic and copies ran while one was open for 0% of the time, Pallas kernels for 2%

profile of v8, /device:TPU:1, one launch (start us, length us, event | category | flops | bytes accessed | tf_op | source)
XLA Modules:
  0.0 79.3 jit_solution(5129804873521287889)
XLA Ops:
  0.0 1.3 %broadcast_in_dim.8 = bf16[32,16,128]{2,1,0:T(8,128)(2,1)} broadcast(bf16[16,128]{1,0:T(8,128)(2,1)} %bitcast.13), dimensions={1,2} | broadcast | bytes 135168 | tf_op jit(solution)/shard_map/broadcast_in_dim | solution.py:262
  1.3 16.6 %all-to-all-start = ((bf16[32,16,128]{2,1,0:T(8,128)(2,1)}), bf16[32,16,128]{2,1,0:T(8,128)(2,1)S(1)}, u32[]{:S(2)}, u32[]{:S(2)}) async-start(bf16[32,16,128]{2,1,0:T(8,128)(2,1)} %broadcast_in_dim.8), calls=%async_computation | async-start | bytes 262144 | tf_op jit(solution)/shard_map/all_to_all | solution.py:263
  18.6 1.9 %stage.1 = (bf16[2,3072,128]{2,1,0:T(8,128)(2,1)S(1)}, bf16[2,3072,128]{2,1,0:T(8,128)(2,1)S(1)}, bf16[2,16,128]{2,1,0:T(8,128)(2,1)S(1)}, bf16[2,16,128]{2,1,0:T(8,128)(2,1)S(1)}, s32[1,16]{1,0:T(1,128)S(1)}) custom-call(bf16[2,3072,128]{2,1,0:T(8,128)(2,1)} %bitcast.9, bf16[2,3072,128]{2,1,0:T(8,128)(2,1)} %bitcast.10, bf16[2,16,128]{2,1,0:T(8,128)(2,1)} %bitcast.11, ...), custom_call_target="tpu_custom_call" | custom-call | bytes 6324288 | tf_op jit(solution)/shard_map/stage/pallas_call | solution.py:184
  20.6 3.5 %all-to-all-done.q_ref = bf16[32,16,128]{2,1,0:T(8,128)(2,1)S(1)} async-done(((bf16[32,16,128]{2,1,0:T(8,128)(2,1)}), bf16[32,16,128]{2,1,0:T(8,128)(2,1)S(1)}, u32[]{:S(2)}, u32[]{:S(2)}) %all-to-all-start) | async-done | bytes 131104 | tf_op jit(solution)/shard_map/all_to_all | solution.py:263
  24.1 2.8 %attend.1 = bf16[8,80,128]{2,1,0:T(8,128)(2,1)S(1)} custom-call(s32[1]{0:T(128)S(6)} %copy.9.length, bf16[32,16,128]{2,1,0:T(8,128)(2,1)S(1)} %all-to-all-done.q_ref, bf16[2,3072,128]{2,1,0:T(8,128)(2,1)S(1)} %get-tuple-element.10.keys, bf16[2,3072,128]{2,1,0:T(8,128)(2,1)S(1)} %get-tuple-element.11.values, ...), custom_call_target="tpu_custom_call" | custom-call | flops 805306368 | bytes 3145728 | tf_op jit(solution)/shard_map/attend/pallas_call | solution.py:201
  27.0 0.0 copy-start
  27.0 7.7 %all_to_all.20.r_ref = bf16[8,80,128]{2,1,0:T(8,128)(2,1)S(1)} all-to-all(bf16[8,80,128]{2,1,0:T(8,128)(2,1)S(1)} %attend.1), channel_id=1, replica_groups={{256,384,0,128,272,400,16,144},{257,385,1,129,273,401,17,145},{258,386,..., dimensions={0} | all-to-all | bytes 327680 | tf_op jit(solution)/shard_map/all_to_all | solution.py:266
  34.6 0.3 combine.1
  34.9 10.3 %all_to_all.21.r_ref = bf16[4,80,128]{2,1,0:T(8,128)(2,1)S(1)} all-to-all(bf16[4,80,128]{2,1,0:T(8,128)(2,1)S(1)} %combine.1), channel_id=1, replica_groups={{64,96,0,32},{65,97,1,33},{66,98,2,34},{67,99,3,35},{68,100,4,36},{69,1..., dimensions={0} | all-to-all | bytes 163840 | tf_op jit(solution)/shard_map/all_to_all | solution.py:268
  45.2 0.3 combine_last.1
  45.5 13.1 %all_to_all.22 = bf16[32,64,128]{2,1,0:T(8,128)(2,1)S(1)} all-to-all(bf16[32,64,128]{2,1,0:T(8,128)(2,1)S(1)} %combine_last.1), channel_id=1, replica_groups={{258,259,256,257,386,387,384,385,2,3,0,1,130,131,128,129,274,275,272,27..., dimensions={0} | all-to-all | bytes 1048576 | tf_op jit(solution)/shard_map/all_to_all | solution.py:272
  58.6 0.0 copy-done
  58.6 0.3 project.1
  58.9 19.8 %all-gather = bf16[16,16,128]{2,1,0:T(8,128)(2,1)S(1)} all-gather(bf16[4,16,128]{2,1,0:T(8,128)(2,1)S(1)} %project.1), channel_id=2, replica_groups={{8,12,0,4},{9,13,1,5},{10,14,2,6},{11,15,3,7},{24,28,16,20},{25,29,17,2..., dimensions={0}, use_global_device_ids=true | all-gather | bytes 81920 | tf_op jit(solution)/shard_map/all_gather | solution.py:274
  78.7 0.6 total.1
Async XLA Ops:
  1.3 22.8 %all-to-all-start = ((bf16[32,16,128]{2,1,0:T(8,128)(2,1)}), bf16[32,16,128]{2,1,0:T(8,128)(2,1)S(1)}, u32[]{:S(2)}, u32[]{:S(2)}) async-start(bf16[32,16,128]{2,1,0:T(8,128)(2,1)} %broadcast_in_dim.8), calls=%async_computation | async-start | bytes 262144 | tf_op jit(solution)/shard_map/all_to_all | solution.py:263
  27.0 31.6 %copy-start = (bf16[4096,128]{1,0:T(8,128)(2,1)S(1)}, bf16[4096,128]{1,0:T(8,128)(2,1)}, u32[]{:S(2)}) copy-start(bf16[4096,128]{1,0:T(8,128)(2,1)} %w_ref.1) | copy-start | bytes 3145732

commit v9 on v8

--- a/solution.py
+++ b/solution.py
@@ -265,7 +265,8 @@
     part = attend(lengths, q, *staged)
     part = lax.all_to_all(part, ("zb", "x"), 0, 0, axis_index_groups=listed(part.shape[0], 2), tiled=True)
     part = combine(part, lax.axis_size("za"), False, rate)
-    part = lax.all_to_all(part, "za", 0, 0, axis_index_groups=listed(part.shape[0], 2), tiled=True)
+    last_first = [[(n - 1) % part.shape[0] for n in range(part.shape[0])]]
+    part = lax.all_to_all(part, "za", 0, 0, axis_index_groups=last_first, tiled=True)
     spread = ("zb", "x", "y")
     sizes = tuple(lax.axis_size(a) for a in spread)
     rows = combine(part, math.prod(sizes), True, rate)

time: 79.7 us -> 79.8 us (level)
  no operation moved by 1% of the time
where the time goes in v9:
time: 79.8 us; the launch traced here: 79.5 us
  blocking collectives  51 us (64%)
  starting transfers between devices  16.6 us (21%)
  Pallas kernels  6.25 us (8%)
  waiting for transfers between devices  3.52 us (4%)
  local copies, waits for them, and re-layouts  1.35 us (2%)
    all_gather x1, blocking collectives, body(): lax.all_gather(out, HEAD, axis=0, axis_index_groups=listed(lax.axis_size(...  19.3 us
    all_to_all x1, starting transfers between devices, body(): lax.all_to_all(sent, Z + ('x',), 0, 0, axis_index_groups=listed(n_ctx, 22...  16.6 us
    all_to_all x1, blocking collectives, body(): lax.all_to_all(rows, spread, 0, 0, axis_index_groups=listed(rows.shape[0]...  13.1 us
    all_to_all x1, blocking collectives, body(): lax.all_to_all(part, 'za', 0, 0, axis_index_groups=last_first, tiled=True)  10.9 us
    all_to_all x1, blocking collectives, body(): lax.all_to_all(part, ('zb', 'x'), 0, 0, axis_index_groups=listed(part.sha...  7.68 us
    all_to_all x1, waiting for transfers between devices, body(): lax.all_to_all(sent, Z + ('x',), 0, 0, axis_index_groups=listed(n_ctx, 22...  3.52 us
    pallas_call x1, Pallas kernels, attend(): pl.pallas_call(functools.partial(attend_kernel, rate=rate, chunk=chunk),...  2.85 us
    pallas_call x1, Pallas kernels, stage(): pl.pallas_call(stage_kernel, out_shape=[jax.ShapeDtypeStruct(a.shape, a.d...  1.94 us
  transfers between devices with their start and end apart: 1, of which 1 were waited for; matrix products, arithmetic and copies ran while one was open for 0% of the time, Pallas kernels for 2%

profile of v9, /device:TPU:1, one launch (start us, length us, event | category | flops | bytes accessed | tf_op | source)
XLA Modules:
  0.0 79.5 jit_solution(13350265704075509902)
XLA Ops:
  0.0 1.3 %broadcast_in_dim.8 = bf16[32,16,128]{2,1,0:T(8,128)(2,1)} broadcast(bf16[16,128]{1,0:T(8,128)(2,1)} %bitcast.13), dimensions={1,2} | broadcast | bytes 135168 | tf_op jit(solution)/shard_map/broadcast_in_dim | solution.py:262
  1.3 16.6 %all-to-all-start = ((bf16[32,16,128]{2,1,0:T(8,128)(2,1)}), bf16[32,16,128]{2,1,0:T(8,128)(2,1)S(1)}, u32[]{:S(2)}, u32[]{:S(2)}) async-start(bf16[32,16,128]{2,1,0:T(8,128)(2,1)} %broadcast_in_dim.8), calls=%async_computation | async-start | bytes 262144 | tf_op jit(solution)/shard_map/all_to_all | solution.py:263
  18.6 1.9 %stage.1 = (bf16[2,3072,128]{2,1,0:T(8,128)(2,1)S(1)}, bf16[2,3072,128]{2,1,0:T(8,128)(2,1)S(1)}, bf16[2,16,128]{2,1,0:T(8,128)(2,1)S(1)}, bf16[2,16,128]{2,1,0:T(8,128)(2,1)S(1)}, s32[1,16]{1,0:T(1,128)S(1)}) custom-call(bf16[2,3072,128]{2,1,0:T(8,128)(2,1)} %bitcast.9, bf16[2,3072,128]{2,1,0:T(8,128)(2,1)} %bitcast.10, bf16[2,16,128]{2,1,0:T(8,128)(2,1)} %bitcast.11, ...), custom_call_target="tpu_custom_call" | custom-call | bytes 6324288 | tf_op jit(solution)/shard_map/stage/pallas_call | solution.py:184
  20.6 3.5 %all-to-all-done.q_ref = bf16[32,16,128]{2,1,0:T(8,128)(2,1)S(1)} async-done(((bf16[32,16,128]{2,1,0:T(8,128)(2,1)}), bf16[32,16,128]{2,1,0:T(8,128)(2,1)S(1)}, u32[]{:S(2)}, u32[]{:S(2)}) %all-to-all-start) | async-done | bytes 131104 | tf_op jit(solution)/shard_map/all_to_all | solution.py:263
  24.1 2.8 %attend.1 = bf16[8,80,128]{2,1,0:T(8,128)(2,1)S(1)} custom-call(s32[1]{0:T(128)S(6)} %copy.9.length, bf16[32,16,128]{2,1,0:T(8,128)(2,1)S(1)} %all-to-all-done.q_ref, bf16[2,3072,128]{2,1,0:T(8,128)(2,1)S(1)} %get-tuple-element.10.keys, bf16[2,3072,128]{2,1,0:T(8,128)(2,1)S(1)} %get-tuple-element.11.values, ...), custom_call_target="tpu_custom_call" | custom-call | flops 805306368 | bytes 3145728 | tf_op jit(solution)/shard_map/attend/pallas_call | solution.py:201
  27.0 0.0 copy-start
  27.0 7.7 %all_to_all.20.r_ref = bf16[8,80,128]{2,1,0:T(8,128)(2,1)S(1)} all-to-all(bf16[8,80,128]{2,1,0:T(8,128)(2,1)S(1)} %attend.1), channel_id=1, replica_groups={{256,384,0,128,272,400,16,144},{257,385,1,129,273,401,17,145},{258,386,..., dimensions={0} | all-to-all | bytes 327680 | tf_op jit(solution)/shard_map/all_to_all | solution.py:266
  34.6 0.3 combine.1
  34.9 10.9 %all_to_all.21.r_ref = bf16[4,80,128]{2,1,0:T(8,128)(2,1)S(1)} all-to-all(bf16[4,80,128]{2,1,0:T(8,128)(2,1)S(1)} %combine.1), channel_id=1, replica_groups={{96,0,32,64},{97,1,33,65},{98,2,34,66},{99,3,35,67},{100,4,36,68},{101,..., dimensions={0} | all-to-all | bytes 163840 | tf_op jit(solution)/shard_map/all_to_all | solution.py:269
  45.8 0.3 combine_last.1
  46.1 13.1 %all_to_all.22 = bf16[32,64,128]{2,1,0:T(8,128)(2,1)S(1)} all-to-all(bf16[32,64,128]{2,1,0:T(8,128)(2,1)S(1)} %combine_last.1), channel_id=1, replica_groups={{258,259,256,257,386,387,384,385,2,3,0,1,130,131,128,129,274,275,272,27..., dimensions={0} | all-to-all | bytes 1048576 | tf_op jit(solution)/shard_map/all_to_all | solution.py:273
  59.2 0.0 copy-done
  59.2 0.3 project.1
  59.5 19.3 %all-gather = bf16[16,16,128]{2,1,0:T(8,128)(2,1)S(1)} all-gather(bf16[4,16,128]{2,1,0:T(8,128)(2,1)S(1)} %project.1), channel_id=2, replica_groups={{8,12,0,4},{9,13,1,5},{10,14,2,6},{11,15,3,7},{24,28,16,20},{25,29,17,2..., dimensions={0}, use_global_device_ids=true | all-gather | bytes 81920 | tf_op jit(solution)/shard_map/all_gather | solution.py:275
  78.9 0.6 total.1
Async XLA Ops:
  1.3 22.8 %all-to-all-start = ((bf16[32,16,128]{2,1,0:T(8,128)(2,1)}), bf16[32,16,128]{2,1,0:T(8,128)(2,1)S(1)}, u32[]{:S(2)}, u32[]{:S(2)}) async-start(bf16[32,16,128]{2,1,0:T(8,128)(2,1)} %broadcast_in_dim.8), calls=%async_computation | async-start | bytes 262144 | tf_op jit(solution)/shard_map/all_to_all | solution.py:263
  27.0 32.3 %copy-start = (bf16[4096,128]{1,0:T(8,128)(2,1)S(1)}, bf16[4096,128]{1,0:T(8,128)(2,1)}, u32[]{:S(2)}) copy-start(bf16[4096,128]{1,0:T(8,128)(2,1)} %w_ref.1) | copy-start | bytes 3145732
